TPU v7x, 512 devices: a whole 4x4x16 slice. The times are simulated.
512 devices in a mesh: rows: 64 (over z, x), cols: 8 (over y, core).
Axes of the slice: x: 4, y: 4, z: 16, core: 2. Of those that a mesh axis runs over, the one named last changes fastest.
Arguments:
- slab: float32 [8192, 16384], P('rows', 'cols'), may hold values from -200 to 200, as said below
Outputs:
- r_rows: float32 [192, 16384], P(None, 'cols')
- updated: float32 [8192, 16384], P('rows', 'cols')
Inputs may be any that keep to these rules, and one draw needn't show every extreme that they name: `slab`: Real-valued activations; every panel has full column rank.
All inputs are finite; a program needn't handle non-finite values.
Results may differ from a plain program's by a relative error of at most 0.0003.
Values sent between devices are 32-bit elements; how exact they have to be, the bound alone decides.
A program may use at most 64 MiB of HBM per device.

v0:
```python
import math

import jax
import jax.numpy as jnp
from jax import lax
from jax.sharding import PartitionSpec as P

PANEL = 64
PANELS = 3


def split_up(value, dim, devices):
    before, after = (value.shape[:dim], value.shape[dim + 1 :])
    return jnp.moveaxis(value.reshape(*before, devices, -1, *after), dim, 0)


def summed_on_arrival(value, axis, dim):
    parts = split_up(value, dim, lax.axis_size(axis))
    arrived = lax.all_to_all(parts, axis, split_axis=0, concat_axis=0, tiled=True)
    return arrived.sum(axis=0)


def padded_to(lines, devices):
    spare = -lines.shape[0] % devices
    if not spare:
        return lines
    return jnp.concatenate([lines, jnp.zeros((spare, *lines.shape[1:]), lines.dtype)])


def from_everyone(value, axis):
    devices = lax.axis_size(axis)
    return lax.all_to_all(
        jnp.broadcast_to(value[None], (devices, *value.shape)), axis, 0, 0, tiled=True
    )


def in_order(parts, dim):
    parts = jnp.moveaxis(parts, 0, dim)
    lengths = parts.shape
    return parts.reshape(*lengths[:dim], lengths[dim] * lengths[dim + 1], *lengths[dim + 2 :])


def gather_directly(value, axis, dim):
    parts = from_everyone(value, axis)
    return in_order(parts, dim)


def total_of(value, axes):
    own = summed_on_arrival(padded_to(value, lax.axis_size(axes)), axes, 0)
    whole = gather_directly(own, axes, 0)
    return whole[: len(value)].reshape(value.shape)


def together(arrays, axis):
    ends = [0]
    for a in arrays:
        ends.append(ends[-1] + a.size)
    subtotal = total_of(jnp.concatenate([a.ravel() for a in arrays]), axis)
    return tuple((subtotal[b:e].reshape(a.shape) for a, b, e in zip(arrays, ends, ends[1:])))


def from_root(value, axis, root):
    return lax.dynamic_index_in_dim(lax.all_gather(value, axis), root, 0, keepdims=False)


def panel_products(earlier, shared):
    return together(
        (
            jnp.dot(earlier.T, shared, precision=lax.Precision.HIGHEST),
            jnp.dot(shared.T, shared, precision=lax.Precision.HIGHEST),
        ),
        "rows",
    )


def on_device(slab):
    rows_here = slab.shape[0]
    col_total = lax.axis_size("cols")
    norm_scale = 1.0 / math.sqrt(rows_here * lax.axis_size("rows"))
    bases = []
    for turn in range(PANELS):
        owner_col = turn % col_total
        offset = turn // col_total * PANEL
        shared = from_root(slab[:, offset : offset + PANEL], "cols", owner_col)
        if bases:
            earlier = jnp.concatenate(bases, 1)
        else:
            earlier = jnp.zeros((rows_here, PANEL), jnp.float32)
        cross, gram_block = panel_products(earlier, shared)
        shared = shared - jnp.dot(earlier, cross, precision=lax.Precision.HIGHEST)
        gram_block = gram_block - jnp.dot(cross.T, cross, precision=lax.Precision.HIGHEST)
        factor = jnp.linalg.cholesky(gram_block)
        bases.append(jax.scipy.linalg.solve_triangular(factor, shared.T, lower=True).T)
    stacked = jnp.concatenate(bases, 1)
    whole, mutual = together(
        (
            jnp.dot(stacked.T, slab, precision=lax.Precision.HIGHEST),
            jnp.dot(stacked.T, stacked, precision=lax.Precision.HIGHEST),
        ),
        "rows",
    )
    coeff_list = []
    for turn in range(PANELS):
        coeffs = whole[turn * PANEL : (turn + 1) * PANEL]
        for older in range(turn):
            coeffs = coeffs - jnp.dot(
                mutual[turn * PANEL : (turn + 1) * PANEL, older * PANEL : (older + 1) * PANEL],
                coeff_list[older],
                precision=lax.Precision.HIGHEST,
            )
        coeff_list.append(coeffs)
    all_coeffs = jnp.concatenate(coeff_list, 0)
    current = slab - jnp.dot(stacked, all_coeffs, precision=lax.Precision.HIGHEST)
    return (all_coeffs * norm_scale, current)


def solution(mesh):
    placed = (P("rows", "cols"),)
    return jax.shard_map(
        on_device,
        mesh=mesh,
        in_specs=placed,
        out_specs=(P(None, "cols"), P("rows", "cols")),
        check_vma=False,
    )
```

profile of v0, /device:TPU:6, one launch (start us, length us, event | category | flops | bytes accessed | tf_op | source)
XLA Modules:
  0.0 376.7 jit_solution(3799119866535331219)
XLA Ops:
  1.5 13.4 %all-gather = f32[1024,64]{0,1:T(8,128)S(1)} all-gather(f32[128,64]{0,1:T(8,128)S(1)} %copy.60), channel_id=2, replica_groups=mesh['rows'=64,'cols'=8] {'cols'}, dimensions={0}, use_global_device_ids=true | all-gather | bytes 294912 | tf_op jit(solution)/shard_map/all_gather | solution.py:63
  15.4 31.0 %all_to_all.60 = f32[64,1,128]{2,1,0:T(1,128)S(1)} all-to-all(f32[64,1,128]{2,1,0:T(1,128)S(1)} %bitcast.61), channel_id=1, replica_groups=mesh['rows'=64,'cols'=8] {'rows'}, dimensions={0} | all-to-all | bytes 65536 | tf_op jit(solution)/shard_map/all_to_all | solution.py:19
  47.1 6.7 %all-to-all-start.1 = ((f32[64,1,128]{2,1,0:T(1,128)}), f32[64,1,128]{2,1,0:T(1,128)S(1)}, u32[]{:S(2)}, u32[]{:S(2)}) async-start(f32[64,1,128]{2,1,0:T(1,128)} %broadcast_in_dim.9), calls=%async_computation.1 | async-start | bytes 65536 | tf_op jit(solution)/shard_map/all_to_all | solution.py:32
  54.1 12.3 %all-to-all-done.1 = f32[64,1,128]{2,1,0:T(1,128)S(1)} async-done(((f32[64,1,128]{2,1,0:T(1,128)}), f32[64,1,128]{2,1,0:T(1,128)S(1)}, u32[]{:S(2)}, u32[]{:S(2)}) %all-to-all-start.1) | async-done | bytes 32800 | tf_op jit(solution)/shard_map/all_to_all | solution.py:32
  67.1 5.8 %cholesky.59 = f32[64,64]{1,0:T(8,128)S(1)} custom-call(f32[64,64]{1,0:T(8,128)S(1)} %fusion.20), custom_call_target="Cholesky" | custom-call | tf_op jit(solution)/shard_map/jit(cholesky)/cholesky | solution.py:92
  74.3 4.9 %custom-call.7 = f32[1,64,64]{1,2,0:T(8,128)S(1)} custom-call(f32[1,64,64]{2,1,0:T(8,128)S(1)} %fusion.7), custom_call_target="InvertDiagBlocksLowerTriangular" | custom-call | tf_op jit(solution)/shard_map/jit(_solve_triangular)/triangular_solve | solution.py:93
  79.7 18.7 %all_to_all.61 = f32[64,1,128]{2,1,0:T(1,128)S(1)} all-to-all(f32[64,1,128]{2,1,0:T(1,128)S(1)} %bitcast.62), channel_id=1, replica_groups=mesh['rows'=64,'cols'=8] {'rows'}, dimensions={0} | all-to-all | bytes 65536 | tf_op jit(solution)/shard_map/all_to_all | solution.py:19
  99.1 6.4 %all-to-all-start.3 = ((f32[64,1,128]{2,1,0:T(1,128)}), f32[64,1,128]{2,1,0:T(1,128)S(1)}, u32[]{:S(2)}, u32[]{:S(2)}) async-start(f32[64,1,128]{2,1,0:T(1,128)} %broadcast_in_dim.10), calls=%async_computation.3 | async-start | bytes 65536 | tf_op jit(solution)/shard_map/all_to_all | solution.py:32
  105.8 12.3 %all-to-all-done.3 = f32[64,1,128]{2,1,0:T(1,128)S(1)} async-done(((f32[64,1,128]{2,1,0:T(1,128)}), f32[64,1,128]{2,1,0:T(1,128)S(1)}, u32[]{:S(2)}, u32[]{:S(2)}) %all-to-all-start.3) | async-done | bytes 32800 | tf_op jit(solution)/shard_map/all_to_all | solution.py:32
  119.1 5.8 %cholesky.70 = f32[64,64]{1,0:T(8,128)S(1)} custom-call(f32[64,64]{1,0:T(8,128)S(1)} %fusion.16), custom_call_target="Cholesky" | custom-call | tf_op jit(solution)/shard_map/jit(cholesky)/cholesky | solution.py:92
  126.3 4.9 %custom-call.8 = f32[1,64,64]{1,2,0:T(8,128)S(1)} custom-call(f32[1,64,64]{2,1,0:T(8,128)S(1)} %fusion.8), custom_call_target="InvertDiagBlocksLowerTriangular" | custom-call | tf_op jit(solution)/shard_map/jit(_solve_triangular)/triangular_solve | solution.py:93
  131.8 19.0 %all_to_all.62 = f32[64,1,192]{2,1,0:T(1,128)S(1)} all-to-all(f32[64,1,192]{2,1,0:T(1,128)S(1)} %all_to_all.46), channel_id=1, replica_groups=mesh['rows'=64,'cols'=8] {'rows'}, dimensions={0} | all-to-all | bytes 98304 | tf_op jit(solution)/shard_map/all_to_all | solution.py:19
  150.9 19.0 %all_to_all.63 = f32[64,1,192]{2,1,0:T(1,128)S(1)} all-to-all(f32[64,1,192]{2,1,0:T(1,128)S(1)} %broadcast_in_dim.11), channel_id=1, replica_groups=mesh['rows'=64,'cols'=8] {'rows'}, dimensions={0} | all-to-all | bytes 98304 | tf_op jit(solution)/shard_map/all_to_all | solution.py:32
  170.9 5.8 %cholesky.81 = f32[64,64]{1,0:T(8,128)S(1)} custom-call(f32[64,64]{1,0:T(8,128)S(1)} %fusion.14), custom_call_target="Cholesky" | custom-call | tf_op jit(solution)/shard_map/jit(cholesky)/cholesky | solution.py:92
  178.1 4.9 %custom-call.9 = f32[1,64,64]{1,2,0:T(8,128)S(1)} custom-call(f32[1,64,64]{2,1,0:T(8,128)S(1)} %fusion.9), custom_call_target="InvertDiagBlocksLowerTriangular" | custom-call | tf_op jit(solution)/shard_map/jit(_solve_triangular)/triangular_solve | solution.py:93
  183.3 1.4 convolution_bitcast_fusion
  187.1 2.1 all_to_all.49
  189.3 84.2 %all_to_all.64 = f32[64,1,6720]{2,1,0:T(1,128)S(1)} all-to-all(f32[64,1,6720]{2,1,0:T(1,128)S(1)} %all_to_all.49), channel_id=1, replica_groups=mesh['rows'=64,'cols'=8] {'rows'}, dimensions={0} | all-to-all | bytes 3440640 | tf_op jit(solution)/shard_map/all_to_all | solution.py:19
  275.5 85.7 %all_to_all.65 = f32[64,1,6720]{2,1,0:T(1,128)S(1)} all-to-all(f32[64,1,6720]{2,1,0:T(1,128)S(1)} %broadcast_in_dim.12), channel_id=1, replica_groups=mesh['rows'=64,'cols'=8] {'rows'}, dimensions={0} | all-to-all | bytes 3440640 | tf_op jit(solution)/shard_map/all_to_all | solution.py:32
  361.2 4.1 %reduce.19 = f32[64,6720]{1,0:T(8,128)S(1)} reduce(f32[64,1,6720]{2,1,0:T(1,128)S(1)} %all_to_all.65, f32[]{:T(128)} %constant.56), dimensions={1}, to_apply=%all_to_all.51.reduce_sub_computation | reduce | bytes 3440644 | tf_op jit(solution)/shard_map/all_to_all | solution.py:32
  365.3 2.5 slice.96
  370.4 1.4 convolution_subtract_fusion.2
  371.9 1.4 convolution_subtract_fusion.1
  373.3 2.1 convolution_subtract_fusion
  (82 shorter events, 19.6 us)
Async XLA Ops:
  47.1 19.3 %all-to-all-start.1 = ((f32[64,1,128]{2,1,0:T(1,128)}), f32[64,1,128]{2,1,0:T(1,128)S(1)}, u32[]{:S(2)}, u32[]{:S(2)}) async-start(f32[64,1,128]{2,1,0:T(1,128)} %broadcast_in_dim.9), calls=%async_computation.1 | async-start | bytes 65536 | tf_op jit(solution)/shard_map/all_to_all | solution.py:32
  79.2 104.1 %copy-start = (f32[128,2048]{1,0:T(8,128)S(1)}, f32[128,2048]{1,0:T(8,128)}, u32[]{:S(2)}) copy-start(f32[128,2048]{1,0:T(8,128)} %param.4) | copy-start | bytes 3145732
  99.1 19.0 %all-to-all-start.3 = ((f32[64,1,128]{2,1,0:T(1,128)}), f32[64,1,128]{2,1,0:T(1,128)S(1)}, u32[]{:S(2)}, u32[]{:S(2)}) async-start(f32[64,1,128]{2,1,0:T(1,128)} %broadcast_in_dim.10), calls=%async_computation.3 | async-start | bytes 65536 | tf_op jit(solution)/shard_map/all_to_all | solution.py:32
  131.4 53.3 %copy-start.2 = (f32[128,64]{0,1:T(8,128)}, f32[128,64]{0,1:T(8,128)S(1)}, u32[]{:S(2)}) copy-start(f32[128,64]{0,1:T(8,128)S(1)} %convolution_bitcast_fusion.2) | copy-start | bytes 98308
  183.2 2.1 copy-start.4
  370.4 2.9 copy-start.1
  370.4 2.9 copy-start.3
  370.4 2.9 copy-start.5
where the time goes:
time: 377 us
  blocking collectives  271 us (72%)
  other arithmetic  44.2 us (12%)
  waiting for transfers between devices  24.7 us (7%)
  starting transfers between devices  13.1 us (3%)
  local copies, waits for them, and re-layouts  11.7 us (3%)
  matrix products  11.1 us (3%)
    all_to_all x4, blocking collectives, summed_on_arrival(): lax.all_to_all(parts, axis, split_axis=0, concat_axis=0, tiled=True)  153 us
    all_to_all x2, blocking collectives, from_everyone(): lax.all_to_all(jnp.broadcast_to(value[None], (devices, *value.shape)), ax...  105 us
    all_to_all x2, waiting for transfers between devices, from_everyone(): lax.all_to_all(jnp.broadcast_to(value[None], (devices, *value.shape)), ax...  24.7 us
    another operation x9, other arithmetic, on_device(): factor = jnp.linalg.cholesky(gram_block)  19.6 us
    another operation x6, other arithmetic, on_device(): jax.scipy.linalg.solve_triangular(factor, shared.T, lower=True)  16.6 us
    all_gather x1, blocking collectives, from_root(): lax.all_gather(value, axis)  13.4 us
    all_to_all x2, starting transfers between devices, from_everyone(): lax.all_to_all(jnp.broadcast_to(value[None], (devices, *value.shape)), ax...  13.1 us
  transfers between devices with their start and end apart: 2, of which 2 were waited for; matrix products, arithmetic and copies ran while one was open for 0% of the time, Pallas kernels for 0%

commit v1 on v0

v1 whole, which is shorter than its diff:
```python
import functools
import math

import jax
import jax.numpy as jnp
from jax import lax
from jax.experimental import pallas as pl
from jax.experimental.pallas import tpu as pltpu
from jax.sharding import PartitionSpec as P

MESH = pl.DeviceIdType.MESH
PANEL = 64
PANELS = 3
N = PANEL * PANELS
F32 = jnp.float32


def dot(a, b, dims=((1,), (0,))):
    return lax.dot_general(
        a, b, (dims, ((), ())), precision=lax.Precision.HIGHEST, preferred_element_type=F32
    )


def dot_t(a, b):
    return dot(a, b, ((1,), (1,)))


def eliminate(s_ref):
    n = PANEL
    lane = lax.broadcasted_iota(jnp.int32, (n, n), 1)
    sub = lax.broadcasted_iota(jnp.int32, (n, n), 0)
    row_lane = lax.broadcasted_iota(jnp.int32, (1, n), 1)
    col_sub = lax.broadcasted_iota(jnp.int32, (n, 1), 0)

    def pick(value, where):
        return jnp.sum(jnp.where(where, value, 0.0), axis=1, keepdims=True)

    def step(i, _):
        j = 2 * i
        s = s_ref[...]
        r0 = s_ref[pl.ds(j, 1), :]
        r1 = s_ref[pl.ds(j + 1, 1), :]
        a = pick(r0, row_lane == j)
        b = pick(r1, row_lane == j)
        d = pick(r1, row_lane == j + 1)
        c0 = pick(s, lane == j)
        c1 = pick(s, lane == j + 1)
        a_inv = 1.0 / a
        ratio = b * a_inv
        second = d - b * ratio
        second_inv = 1.0 / second
        r0m = jnp.where(row_lane == j, 1.0, r0)
        r1n = jnp.where(row_lane == j, 0.0, r1) - ratio * r0m
        r0u = jnp.where(row_lane == j + 1, 0.0, r0m) * a_inv
        r1u = jnp.where(row_lane == j + 1, 1.0, r1n) * second_inv
        r1s = jnp.where(row_lane == j + 1, second, r1n)
        below = col_sub > j + 1
        c0b = jnp.where(below, c0, 0.0)
        c1b = jnp.where(below, c1 - c0 * ratio, 0.0)
        base = jnp.where((lane >= j) & (lane <= j + 1) & (sub > j + 1), 0.0, s)
        s_ref[...] = jnp.where(sub == j + 1, r1s, base - c0b * r0u - c1b * r1u)
        return 0

    lax.fori_loop(0, n // 2, step, 0)
    s = s_ref[...]
    pivots = pick(s, lane == sub)
    return jnp.where(lane < sub, s, jnp.where(lane == sub, 1.0, 0.0)) * (1.0 / jnp.sqrt(pivots))


def kernel(
    slab, r_out, u_out,
    at, gp, g1, g2, g3, gfull,
    mx, mz, rx1, rz1a, rz1b, rz1c, px, pz, rx2a, rx2b, rx2c, rz2, rr, mfx, mfz,
    s_ref, l_ref, t_ref, q_ref,
    p_send, p_recv, sends, recvs,
):
    row, col = lax.axis_index("rows"), lax.axis_index("cols")
    z, x = row // 4, row % 4
    zhi, zlo = z // 4, z % 4

    def at_z(dz):
        return (((z + dz + 16) % 16) * 4 + x, col)

    def at_x(d):
        return (z * 4 + (x + d) % 4, col)

    def at_col(d):
        return (row, (col + d) % 8)

    z_peers = (1, -1, 2, -2, 3, -3, 4, -4, 8)
    peers = [at_z(d) for d in z_peers] + [at_x(d) for d in (1, 2, 3)] + [at_col(d) for d in range(1, 8)]
    barrier = pltpu.get_barrier_semaphore()
    for peer in peers:
        pl.semaphore_signal(barrier, inc=1, device_id=peer, device_id_type=MESH)
    pl.semaphore_wait(barrier, len(peers))

    started = []

    def send(src, dst, peer):
        i = len(started)
        copy = pltpu.make_async_remote_copy(
            src_ref=src, dst_ref=dst, send_sem=sends.at[i], recv_sem=recvs.at[i],
            device_id=peer, device_id_type=MESH,
        )
        copy.start()
        started.append(copy)
        return copy

    def arrived(copies):
        for copy in copies:
            copy.wait_recv()

    def panel_copy(owner, d):
        rows = at.at[pl.ds(pl.multiple_of(owner * PANEL, PANEL), PANEL)]
        return pltpu.make_async_remote_copy(
            src_ref=rows, dst_ref=rows, send_sem=p_send.at[d - 1], recv_sem=p_recv.at[owner],
            device_id=at_col(d), device_id_type=MESH,
        )

    @pl.when(col < PANELS)
    def _():
        at[pl.ds(pl.multiple_of(col * PANEL, PANEL), PANEL), :] = slab[:, 0:128].T[:PANEL]
        for d in (4, 3, 5, 2, 6, 7, 1):
            panel_copy(col, d).start()

    for k in range(PANELS):
        @pl.when(col != k)
        def _():
            panel_copy(k, 1).wait_recv()

    panels_t = at[...]

    gp[0:24] = dot_t(panels_t, panels_t[0:128]).reshape(24, 8, 128)
    gp[24:32] = dot_t(panels_t[128:192], jnp.concatenate([panels_t[128:192], panels_t[128:192]], 0)).reshape(8, 8, 128)
    mine = 4 * col + x
    c_g1 = [send(gp.at[4 * col + (x + d) % 4], g1.at[d - 1], at_x(d)) for d in (2, 1, 3)]

    for q in range(4):
        mz[:, 256 * q:256 * q + 256] = dot(panels_t, slab[:, 1024 + 256 * q:1280 + 256 * q])

    def around_z(piece, half_a, half_b, dst, dst_a, dst_b):
        far = (zlo + 2) % 4
        return [
            send(half_a(far), dst_a, at_z(2)),
            send(half_b(far), dst_b, at_z(-2)),
            send(piece((zlo + 1) % 4), dst[0], at_z(1)),
            send(piece((zlo + 3) % 4), dst[1], at_z(-1)),
        ]

    def rows48(i):
        return pl.ds(pl.multiple_of(48 * i, 8), 48)

    def rows24(i, half):
        return pl.ds(pl.multiple_of(48 * i + 24 * half, 8), 24)

    c_z1 = around_z(
        lambda i: mz.at[rows48(i)], lambda i: mz.at[rows24(i, 0)], lambda i: mz.at[rows24(i, 1)],
        (rz1a, rz1b), rz1c.at[0:24], rz1c.at[24:48],
    )
    c_x1 = []
    for d in (2, 1, 3, 0):
        chunk = (x + d) % 4
        mx[chunk] = dot(panels_t, slab[:, pl.ds(pl.multiple_of(256 * chunk, 256), 256)])
        if d:
            c_x1.append(send(mx.at[chunk], rx1.at[d - 1], at_x(d)))

    arrived(c_g1)
    g2[zlo] = gp[mine] + g1[0] + g1[1] + g1[2]
    c_g2 = [
        send(g2.at[zlo], g2.at[zlo], ((zhi * 4 + (zlo + e) % 4) * 4 + x, col)) for e in (2, 1, 3)
    ]

    arrived(c_z1)
    for q in range(4):
        cols = slice(256 * q, 256 * q + 256)
        pz[q] = mz[rows48(zlo), cols] + rz1a[:, cols] + rz1b[:, cols] + rz1c[:, cols]
    arrived(c_g2)
    g3[zhi] = g2[0] + g2[1] + g2[2] + g2[3]
    c_g3 = [send(g3.at[zhi], g3.at[zhi], at_z(4 * e)) for e in (2, 1, 3)]
    c_z2 = [send(pz.at[(x + d) % 4], rz2.at[d - 1], at_x(d)) for d in (2, 1, 3)]

    arrived(c_x1)
    px[...] = mx[x] + rx1[0] + rx1[1] + rx1[2]
    c_x2 = around_z(
        lambda i: px.at[rows48(i)], lambda i: px.at[rows24(i, 0)], lambda i: px.at[rows24(i, 1)],
        (rx2a, rx2b), rx2c.at[0:24], rx2c.at[24:48],
    )

    arrived(c_z2)
    rr[1, zhi] = pz[x] + rz2[0] + rz2[1] + rz2[2]
    c_z3 = [send(rr.at[1, zhi], rr.at[1, zhi], at_z(4 * e)) for e in (2, 1, 3)]
    arrived(c_x2)
    rr[0, zhi] = px[rows48(zlo), :] + rx2a[...] + rx2b[...] + rx2c[...]
    c_x3 = [send(rr.at[0, zhi], rr.at[0, zhi], at_z(4 * e)) for e in (2, 1, 3)]

    arrived(c_g3)
    gfull[mine] = g3[0] + g3[1] + g3[2] + g3[3]
    c_g4 = [send(gfull.at[mine], gfull.at[mine], at_x(d)) for d in (2, 1, 3)]
    arrived(c_g4)
    four = gfull.at[pl.ds(4 * col, 4)]
    c_g5 = [send(four, four, at_col(d)) for d in (4, 3, 5, 2, 6, 7, 1)]
    arrived(c_g5)

    def block(i, j):
        if j == 2:
            return gfull[24:32].reshape(64, 128)[:, 0:64]
        return gfull[8 * i:8 * i + 8].reshape(64, 128)[:, 64 * j:64 * j + 64]

    t_ref[...] = jnp.zeros_like(t_ref)
    s_ref[...] = block(0, 0)
    t00 = eliminate(s_ref)
    l10, l20 = dot_t(block(1, 0), t00), dot_t(block(2, 0), t00)
    t_ref[0:64, 0:64] = t00
    l_ref[0], l_ref[1] = l10, l20
    s_ref[...] = block(1, 1) - dot_t(l10, l10)
    l_ref[2] = block(2, 1) - dot_t(l20, l10)
    l_ref[3] = block(2, 2) - dot_t(l20, l20)

    arrived(c_z3)
    wz = rr[1, 0] + rr[1, 1] + rr[1, 2] + rr[1, 3]
    mfz[x, rows48(zlo), :] = wz
    own = mfz.at[x, rows48(zlo)]
    c_z4 = [send(own, own, at_x(d)) for d in (2, 1, 3)]
    arrived(c_x3)
    mfx[x, rows48(zlo), :] = rr[0, 0] + rr[0, 1] + rr[0, 2] + rr[0, 3]

    def own_rows(ref):
        return around_z(
            lambda i: ref.at[rows48(zlo)], lambda i: ref.at[rows24(zlo, 0)], lambda i: ref.at[rows24(zlo, 1)],
            (ref.at[rows48(zlo)], ref.at[rows48(zlo)]), ref.at[rows24(zlo, 0)], ref.at[rows24(zlo, 1)],
        )

    c_x4 = own_rows(mfx.at[x])

    t11 = eliminate(s_ref)
    t_ref[64:128, 64:128] = t11
    l21 = dot_t(l_ref[2], t11)
    l_ref[2] = l21
    s_ref[...] = l_ref[3] - dot_t(l21, l21)

    arrived(c_z4)
    c_z5 = []
    far = mfz.at[:, rows24(zlo, 0)]
    c_z5.append(send(far, far, at_z(2)))
    far = mfz.at[:, rows24(zlo, 1)]
    c_z5.append(send(far, far, at_z(-2)))
    near = mfz.at[:, rows48(zlo)]
    c_z5.append(send(near, near, at_z(1)))
    c_z5.append(send(near, near, at_z(-1)))
    arrived(c_x4)
    c_x5 = [send(mfx.at[x], mfx.at[x], at_x(d)) for d in (2, 1, 3)]

    t22 = eliminate(s_ref)
    t00, t11 = t_ref[0:64, 0:64], t_ref[64:128, 64:128]
    l10, l20, l21 = l_ref[0], l_ref[1], l_ref[2]
    t10 = -dot(t11, dot(l10, t00))
    t_ref[64:128, 0:64] = t10
    t_ref[128:192, 0:64] = -dot(t22, dot(l20, t00) + dot(l21, t10))
    t_ref[128:192, 64:128] = -dot(t22, dot(l21, t11))
    t_ref[128:192, 128:192] = t22
    q_ref[...] = dot(t_ref[...], at[...]).T

    norm_scale = 1.0 / math.sqrt(128 * 64)

    def finish(chunk, first):
        cols = pl.ds(pl.multiple_of(first, 256), 256)
        coeffs = dot(t_ref[...], chunk)
        r_out[:, cols] = coeffs * norm_scale
        u_out[:, cols] = slab[:, cols] - dot(q_ref[...], coeffs)

    finish(mfx[x], 256 * x)
    for d, copy in zip((2, 1, 3), c_x5):
        copy.wait_recv()
    for d in (1, 2, 3):
        chunk = (x + d) % 4
        finish(mfx[chunk], 256 * chunk)
    arrived(c_z5)
    for q in range(4):
        finish(mfz[q], 1024 + 256 * q)

    for copy in started:
        copy.wait_send()

    @pl.when(col < PANELS)
    def _():
        for d in range(1, 8):
            panel_copy(col, d).wait_send()


MESSAGES = 53


def on_device(slab):
    vmem = pl.BlockSpec(memory_space=pltpu.VMEM)

    def buf(*shape):
        return pltpu.VMEM(shape, F32)

    return pl.pallas_call(
        kernel,
        out_shape=(
            jax.ShapeDtypeStruct((N, 2048), F32),
            jax.ShapeDtypeStruct((128, 2048), F32),
        ),
        in_specs=[vmem],
        out_specs=(vmem, vmem),
        scratch_shapes=[
            buf(N, 128), buf(32, 8, 128), buf(3, 8, 128), buf(4, 8, 128), buf(4, 8, 128), buf(32, 8, 128),
            buf(4, N, 256), buf(N, 1024), buf(3, N, 256), buf(48, 1024), buf(48, 1024), buf(48, 1024),
            buf(N, 256), buf(4, 48, 256), buf(48, 256), buf(48, 256), buf(48, 256), buf(3, 48, 256),
            buf(2, 4, 48, 256), buf(4, N, 256), buf(4, N, 256),
            buf(64, 64), buf(4, 64, 64), buf(N, N), buf(128, N),
            pltpu.SemaphoreType.DMA((7,)), pltpu.SemaphoreType.DMA((PANELS,)),
            pltpu.SemaphoreType.DMA((MESSAGES,)), pltpu.SemaphoreType.DMA((MESSAGES,)),
        ],
        compiler_params=pltpu.CompilerParams(
            collective_id=0, has_side_effects=True, vmem_limit_bytes=40 << 20
        ),
    )(slab)


def solution(mesh):
    return jax.shard_map(
        on_device,
        mesh=mesh,
        in_specs=(P("rows", "cols"),),
        out_specs=(P(None, "cols"), P("rows", "cols")),
        check_vma=False,
    )
```

time: 377 us -> 85.8 us (0.23)
  the two profiles are of different devices: /device:TPU:6 before, /device:TPU:1 now
where the time goes in v1:
time: 85.8 us; the launch traced here: 85.6 us
  Pallas kernels  81.7 us (95%)
  local copies, waits for them, and re-layouts  3.33 us (4%)
    pallas_call x1, Pallas kernels, on_device(): pl.pallas_call(kernel, out_shape=(jax.ShapeDtypeStruct((N, 2048), F32), j...  81.7 us
    unnamed x4, local copies, waits for them, and re-layouts  3.33 us

profile of v1, /device:TPU:1, one launch (start us, length us, event | category | flops | bytes accessed | tf_op | source)
XLA Modules:
  0.0 85.6 jit_solution(13879287023555655770)
XLA Ops:
  0.6 0.0 copy-start
  0.6 1.2 %copy-done = f32[128,2048]{1,0:T(8,128)S(1)} copy-done((f32[128,2048]{1,0:T(8,128)S(1)}, f32[128,2048]{1,0:T(8,128)}, u32[]{:S(2)}) %copy-start) | copy-done | bytes 1048600
  1.9 81.7 %shard_map.30 = (f32[192,2048]{1,0:T(8,128)S(1)}, f32[128,2048]{1,0:T(8,128)S(1)}) custom-call(f32[128,2048]{1,0:T(8,128)S(1)} %copy-done), custom_call_target="tpu_custom_call" | custom-call | tf_op jit(solution)/shard_map/pallas_call | solution.py:299
  83.5 1.1 %copy.5 = f32[192,2048]{1,0:T(8,128)} copy(f32[192,2048]{1,0:T(8,128)S(1)} %get-tuple-element.4) | data formatting | bytes 3145728
  84.7 1.0 %copy.6 = f32[128,2048]{1,0:T(8,128)} copy(f32[128,2048]{1,0:T(8,128)S(1)} %get-tuple-element.5) | data formatting | bytes 2097152
Async XLA Ops:
  0.6 1.2 %copy-start = (f32[128,2048]{1,0:T(8,128)S(1)}, f32[128,2048]{1,0:T(8,128)}, u32[]{:S(2)}) copy-start(f32[128,2048]{1,0:T(8,128)} %slab.1) | copy-start | bytes 3145732

commit v2 on v1

--- a/solution.py
+++ b/solution.py
@@ -68,11 +68,11 @@
 
 
 def kernel(
-    slab, r_out, u_out,
-    at, gp, g1, g2, g3, gfull,
+    slab_hbm, r_out, u_out,
+    slab, r_buf, u_buf, at, gp, g1, g2, g3, gfull,
     mx, mz, rx1, rz1a, rz1b, rz1c, px, pz, rx2a, rx2b, rx2c, rz2, rr, mfx, mfz,
     s_ref, l_ref, t_ref, q_ref,
-    p_send, p_recv, sends, recvs,
+    p_send, p_recv, sends, recvs, in_sem, out_sem, far1, far2,
 ):
     row, col = lax.axis_index("rows"), lax.axis_index("cols")
     z, x = row // 4, row % 4
@@ -87,12 +87,20 @@
     def at_col(d):
         return (row, (col + d) % 8)
 
-    z_peers = (1, -1, 2, -2, 3, -3, 4, -4, 8)
+    first = pltpu.make_async_copy(slab_hbm.at[:, 0:256], slab.at[:, 0:256], in_sem.at[0])
+    rest = pltpu.make_async_copy(slab_hbm.at[:, 256:2048], slab.at[:, 256:2048], in_sem.at[1])
+    first.start()
+    rest.start()
+
+    z_peers = (1, -1, 2, -2, 3, -3)
     peers = [at_z(d) for d in z_peers] + [at_x(d) for d in (1, 2, 3)] + [at_col(d) for d in range(1, 8)]
     barrier = pltpu.get_barrier_semaphore()
     for peer in peers:
         pl.semaphore_signal(barrier, inc=1, device_id=peer, device_id_type=MESH)
     pl.semaphore_wait(barrier, len(peers))
+    for d in (2, -2):
+        pl.semaphore_signal(far1, inc=1, device_id=at_z(d), device_id_type=MESH)
+    first.wait()
 
     started = []
 
@@ -123,6 +131,10 @@
         for d in (4, 3, 5, 2, 6, 7, 1):
             panel_copy(col, d).start()
 
+    pl.semaphore_wait(far1, 2)
+    for d in (4, -4):
+        pl.semaphore_signal(far2, inc=1, device_id=at_z(d), device_id_type=MESH)
+    rest.wait()
     for k in range(PANELS):
         @pl.when(col != k)
         def _():
@@ -176,6 +188,7 @@
         pz[q] = mz[rows48(zlo), cols] + rz1a[:, cols] + rz1b[:, cols] + rz1c[:, cols]
     arrived(c_g2)
     g3[zhi] = g2[0] + g2[1] + g2[2] + g2[3]
+    pl.semaphore_wait(far2, 2)
     c_g3 = [send(g3.at[zhi], g3.at[zhi], at_z(4 * e)) for e in (2, 1, 3)]
     c_z2 = [send(pz.at[(x + d) % 4], rz2.at[d - 1], at_x(d)) for d in (2, 1, 3)]
 
@@ -200,6 +213,22 @@
     four = gfull.at[pl.ds(4 * col, 4)]
     c_g5 = [send(four, four, at_col(d)) for d in (4, 3, 5, 2, 6, 7, 1)]
     arrived(c_g5)
+
+    arrived(c_z3)
+    wz = rr[1, 0] + rr[1, 1] + rr[1, 2] + rr[1, 3]
+    mfz[x, rows48(zlo), :] = wz
+    own = mfz.at[x, rows48(zlo)]
+    c_z4 = [send(own, own, at_x(d)) for d in (2, 1, 3)]
+    arrived(c_x3)
+    mfx[x, rows48(zlo), :] = rr[0, 0] + rr[0, 1] + rr[0, 2] + rr[0, 3]
+
+    def own_rows(ref, at_rows):
+        whole, half_a, half_b = (at_rows(ref, rows) for rows in (rows48(zlo), rows24(zlo, 0), rows24(zlo, 1)))
+        return around_z(
+            lambda i: whole, lambda i: half_a, lambda i: half_b, (whole, whole), half_a, half_b
+        )
+
+    c_x4 = own_rows(mfx.at[x], lambda ref, rows: ref.at[rows])
 
     def block(i, j):
         if j == 2:
@@ -216,39 +245,18 @@
     l_ref[2] = block(2, 1) - dot_t(l20, l10)
     l_ref[3] = block(2, 2) - dot_t(l20, l20)
 
-    arrived(c_z3)
-    wz = rr[1, 0] + rr[1, 1] + rr[1, 2] + rr[1, 3]
-    mfz[x, rows48(zlo), :] = wz
-    own = mfz.at[x, rows48(zlo)]
-    c_z4 = [send(own, own, at_x(d)) for d in (2, 1, 3)]
-    arrived(c_x3)
-    mfx[x, rows48(zlo), :] = rr[0, 0] + rr[0, 1] + rr[0, 2] + rr[0, 3]
-
-    def own_rows(ref):
-        return around_z(
-            lambda i: ref.at[rows48(zlo)], lambda i: ref.at[rows24(zlo, 0)], lambda i: ref.at[rows24(zlo, 1)],
-            (ref.at[rows48(zlo)], ref.at[rows48(zlo)]), ref.at[rows24(zlo, 0)], ref.at[rows24(zlo, 1)],
-        )
-
-    c_x4 = own_rows(mfx.at[x])
+    arrived(c_z4)
+    c_z5 = []
+    for half in (slice(0, 2), slice(2, 4)):
+        c_z5.append(own_rows(mfz.at[half], lambda ref, rows: ref.at[:, rows]))
+    arrived(c_x4)
+    c_x5 = [send(mfx.at[x], mfx.at[x], at_x(d)) for d in (2, 1, 3)]
 
     t11 = eliminate(s_ref)
     t_ref[64:128, 64:128] = t11
     l21 = dot_t(l_ref[2], t11)
     l_ref[2] = l21
     s_ref[...] = l_ref[3] - dot_t(l21, l21)
-
-    arrived(c_z4)
-    c_z5 = []
-    far = mfz.at[:, rows24(zlo, 0)]
-    c_z5.append(send(far, far, at_z(2)))
-    far = mfz.at[:, rows24(zlo, 1)]
-    c_z5.append(send(far, far, at_z(-2)))
-    near = mfz.at[:, rows48(zlo)]
-    c_z5.append(send(near, near, at_z(1)))
-    c_z5.append(send(near, near, at_z(-1)))
-    arrived(c_x4)
-    c_x5 = [send(mfx.at[x], mfx.at[x], at_x(d)) for d in (2, 1, 3)]
 
     t22 = eliminate(s_ref)
     t00, t11 = t_ref[0:64, 0:64], t_ref[64:128, 64:128]
@@ -262,22 +270,31 @@
 
     norm_scale = 1.0 / math.sqrt(128 * 64)
 
+    outs = []
+
     def finish(chunk, first):
+        i = len(outs) // 2
         cols = pl.ds(pl.multiple_of(first, 256), 256)
         coeffs = dot(t_ref[...], chunk)
-        r_out[:, cols] = coeffs * norm_scale
-        u_out[:, cols] = slab[:, cols] - dot(q_ref[...], coeffs)
+        r_buf[i] = coeffs * norm_scale
+        outs.append(pltpu.make_async_copy(r_buf.at[i], r_out.at[:, cols], out_sem.at[2 * i]))
+        outs[-1].start()
+        u_buf[i] = slab[:, cols] - dot(q_ref[...], coeffs)
+        outs.append(pltpu.make_async_copy(u_buf.at[i], u_out.at[:, cols], out_sem.at[2 * i + 1]))
+        outs[-1].start()
 
     finish(mfx[x], 256 * x)
-    for d, copy in zip((2, 1, 3), c_x5):
-        copy.wait_recv()
-    for d in (1, 2, 3):
-        chunk = (x + d) % 4
+    for half in range(2):
+        arrived(c_z5[half])
+        for q in (2 * half, 2 * half + 1):
+            finish(mfz[q], 1024 + 256 * q)
+    for i, d in ((1, 1), (2, 3), (0, 2)):
+        c_x5[i].wait_recv()
+        chunk = (x + 4 - d) % 4
         finish(mfx[chunk], 256 * chunk)
-    arrived(c_z5)
-    for q in range(4):
-        finish(mfz[q], 1024 + 256 * q)
-
+
+    for copy in outs:
+        copy.wait()
     for copy in started:
         copy.wait_send()
 
@@ -287,11 +304,12 @@
             panel_copy(col, d).wait_send()
 
 
-MESSAGES = 53
+MESSAGES = 57
 
 
 def on_device(slab):
-    vmem = pl.BlockSpec(memory_space=pltpu.VMEM)
+    hbm = pl.BlockSpec(memory_space=pltpu.HBM)
+    place = pl.BlockSpec(memory_space=pl.ANY)
 
     def buf(*shape):
         return pltpu.VMEM(shape, F32)
@@ -302,19 +320,21 @@
             jax.ShapeDtypeStruct((N, 2048), F32),
             jax.ShapeDtypeStruct((128, 2048), F32),
         ),
-        in_specs=[vmem],
-        out_specs=(vmem, vmem),
+        in_specs=[hbm],
+        out_specs=(place, place),
         scratch_shapes=[
-            buf(N, 128), buf(32, 8, 128), buf(3, 8, 128), buf(4, 8, 128), buf(4, 8, 128), buf(32, 8, 128),
+            buf(128, 2048), buf(8, N, 256), buf(8, 128, 256), buf(N, 128), buf(32, 8, 128), buf(3, 8, 128), buf(4, 8, 128), buf(4, 8, 128), buf(32, 8, 128),
             buf(4, N, 256), buf(N, 1024), buf(3, N, 256), buf(48, 1024), buf(48, 1024), buf(48, 1024),
             buf(N, 256), buf(4, 48, 256), buf(48, 256), buf(48, 256), buf(48, 256), buf(3, 48, 256),
             buf(2, 4, 48, 256), buf(4, N, 256), buf(4, N, 256),
             buf(64, 64), buf(4, 64, 64), buf(N, N), buf(128, N),
             pltpu.SemaphoreType.DMA((7,)), pltpu.SemaphoreType.DMA((PANELS,)),
             pltpu.SemaphoreType.DMA((MESSAGES,)), pltpu.SemaphoreType.DMA((MESSAGES,)),
+            pltpu.SemaphoreType.DMA((2,)), pltpu.SemaphoreType.DMA((16,)),
+            pltpu.SemaphoreType.REGULAR, pltpu.SemaphoreType.REGULAR,
         ],
         compiler_params=pltpu.CompilerParams(
-            collective_id=0, has_side_effects=True, vmem_limit_bytes=40 << 20
+            collective_id=0, has_side_effects=True, vmem_limit_bytes=48 << 20
         ),
     )(slab)
 

time: 85.8 us -> 82.4 us (0.960)
  Pallas kernels: 81.7 us -> 78.2 us
    pallas_call x1, Pallas kernels: 81.7 us -> 78.2 us  [on_device(): pl.pallas_call(kernel, out_shape=(jax.ShapeDtypeStruct((N, 2048), F32), j...]
where the time goes in v2:
time: 82.4 us; the launch traced here: 82.2 us
  Pallas kernels  78.2 us (95%)
  local copies, waits for them, and re-layouts  3.33 us (4%)
    pallas_call x1, Pallas kernels, on_device(): pl.pallas_call(kernel, out_shape=(jax.ShapeDtypeStruct((N, 2048), F32), j...  78.2 us
    unnamed x4, local copies, waits for them, and re-layouts  3.33 us

profile of v2, /device:TPU:1, one launch (start us, length us, event | category | flops | bytes accessed | tf_op | source)
XLA Modules:
  0.0 82.2 jit_solution(11937152727948861918)
XLA Ops:
  0.6 0.0 copy-start
  0.6 1.2 %copy-done = f32[128,2048]{1,0:T(8,128)S(1)} copy-done((f32[128,2048]{1,0:T(8,128)S(1)}, f32[128,2048]{1,0:T(8,128)}, u32[]{:S(2)}) %copy-start) | copy-done | bytes 1048600
  1.9 78.2 %shard_map.30 = (f32[192,2048]{1,0:T(8,128)S(1)}, f32[128,2048]{1,0:T(8,128)S(1)}) custom-call(f32[128,2048]{1,0:T(8,128)S(1)} %copy-done), custom_call_target="tpu_custom_call" | custom-call | tf_op jit(solution)/shard_map/pallas_call | solution.py:317
  80.1 1.1 %copy.5 = f32[192,2048]{1,0:T(8,128)} copy(f32[192,2048]{1,0:T(8,128)S(1)} %get-tuple-element.4) | data formatting | bytes 3145728
  81.2 1.0 %copy.6 = f32[128,2048]{1,0:T(8,128)} copy(f32[128,2048]{1,0:T(8,128)S(1)} %get-tuple-element.5) | data formatting | bytes 2097152
Async XLA Ops:
  0.6 1.2 %copy-start = (f32[128,2048]{1,0:T(8,128)S(1)}, f32[128,2048]{1,0:T(8,128)}, u32[]{:S(2)}) copy-start(f32[128,2048]{1,0:T(8,128)} %slab_hbm.1) | copy-start | bytes 3145732

commit v3 on v2

--- a/solution.py
+++ b/solution.py
@@ -69,8 +69,8 @@
 
 def kernel(
     slab_hbm, r_out, u_out,
-    slab, r_buf, u_buf, at, gp, g1, g2, g3, gfull,
-    mx, mz, rx1, rz1a, rz1b, rz1c, px, pz, rx2a, rx2b, rx2c, rz2, rr, mfx, mfz,
+    slab, r_buf, u_buf, at, gp, g1, g2, gfull,
+    mx, mz, rx1, rz1a, rz1b, rz1c, px, pz, rx2a, rx2b, rx2c, rz2, rr, mfx, mfz, cx,
     s_ref, l_ref, t_ref, q_ref,
     p_send, p_recv, sends, recvs, in_sem, out_sem, far1, far2,
 ):
@@ -92,7 +92,7 @@
     first.start()
     rest.start()
 
-    z_peers = (1, -1, 2, -2, 3, -3)
+    z_peers = (1, -1, 2, -2)
     peers = [at_z(d) for d in z_peers] + [at_x(d) for d in (1, 2, 3)] + [at_col(d) for d in range(1, 8)]
     barrier = pltpu.get_barrier_semaphore()
     for peer in peers:
@@ -147,9 +147,6 @@
     mine = 4 * col + x
     c_g1 = [send(gp.at[4 * col + (x + d) % 4], g1.at[d - 1], at_x(d)) for d in (2, 1, 3)]
 
-    for q in range(4):
-        mz[:, 256 * q:256 * q + 256] = dot(panels_t, slab[:, 1024 + 256 * q:1280 + 256 * q])
-
     def around_z(piece, half_a, half_b, dst, dst_a, dst_b):
         far = (zlo + 2) % 4
         return [
@@ -165,32 +162,33 @@
     def rows24(i, half):
         return pl.ds(pl.multiple_of(48 * i + 24 * half, 8), 24)
 
-    c_z1 = around_z(
-        lambda i: mz.at[rows48(i)], lambda i: mz.at[rows24(i, 0)], lambda i: mz.at[rows24(i, 1)],
-        (rz1a, rz1b), rz1c.at[0:24], rz1c.at[24:48],
-    )
+    def first_z(half):
+        for q in (2 * half, 2 * half + 1):
+            mz[:, 256 * q:256 * q + 256] = dot(panels_t, slab[:, 1024 + 256 * q:1280 + 256 * q])
+
+    def send_z(half):
+        cols = slice(512 * half, 512 * half + 512)
+        return around_z(
+            lambda i: mz.at[rows48(i), cols], lambda i: mz.at[rows24(i, 0), cols],
+            lambda i: mz.at[rows24(i, 1), cols],
+            (rz1a.at[:, cols], rz1b.at[:, cols]), rz1c.at[0:24, cols], rz1c.at[24:48, cols],
+        )
+
+    first_z(0)
+    c_z1 = send_z(0)
     c_x1 = []
     for d in (2, 1, 3, 0):
         chunk = (x + d) % 4
         mx[chunk] = dot(panels_t, slab[:, pl.ds(pl.multiple_of(256 * chunk, 256), 256)])
         if d:
             c_x1.append(send(mx.at[chunk], rx1.at[d - 1], at_x(d)))
+    first_z(1)
 
     arrived(c_g1)
-    g2[zlo] = gp[mine] + g1[0] + g1[1] + g1[2]
-    c_g2 = [
-        send(g2.at[zlo], g2.at[zlo], ((zhi * 4 + (zlo + e) % 4) * 4 + x, col)) for e in (2, 1, 3)
-    ]
-
-    arrived(c_z1)
-    for q in range(4):
-        cols = slice(256 * q, 256 * q + 256)
-        pz[q] = mz[rows48(zlo), cols] + rz1a[:, cols] + rz1b[:, cols] + rz1c[:, cols]
-    arrived(c_g2)
-    g3[zhi] = g2[0] + g2[1] + g2[2] + g2[3]
+    g2[z] = gp[mine] + g1[0] + g1[1] + g1[2]
     pl.semaphore_wait(far2, 2)
-    c_g3 = [send(g3.at[zhi], g3.at[zhi], at_z(4 * e)) for e in (2, 1, 3)]
-    c_z2 = [send(pz.at[(x + d) % 4], rz2.at[d - 1], at_x(d)) for d in (2, 1, 3)]
+    c_g2 = [send(g2.at[z], g2.at[z], at_z(d)) for d in (8, 7, 9, 6, 10, 5, 11, 4, 12, 3, 13, 2, 14, 1, 15)]
+    c_z1 += send_z(1)
 
     arrived(c_x1)
     px[...] = mx[x] + rx1[0] + rx1[1] + rx1[2]
@@ -198,37 +196,27 @@
         lambda i: px.at[rows48(i)], lambda i: px.at[rows24(i, 0)], lambda i: px.at[rows24(i, 1)],
         (rx2a, rx2b), rx2c.at[0:24], rx2c.at[24:48],
     )
-
+    arrived(c_g2)
+    total = g2[0]
+    for i in range(1, 16):
+        total = total + g2[i]
+    gfull[mine] = total
+    c_g4 = [send(gfull.at[mine], gfull.at[mine], at_x(d)) for d in (2, 1, 3)]
+    arrived(c_z1)
+    for q in range(4):
+        cols = slice(256 * q, 256 * q + 256)
+        pz[q] = mz[rows48(zlo), cols] + rz1a[:, cols] + rz1b[:, cols] + rz1c[:, cols]
+    c_z2 = [send(pz.at[(x + d) % 4], rz2.at[d - 1], at_x(d)) for d in (2, 1, 3)]
+    arrived(c_g4)
+    four = gfull.at[pl.ds(4 * col, 4)]
+    c_g5 = [send(four, four, at_col(d)) for d in (4, 3, 5, 2, 6, 7, 1)]
+    arrived(c_x2)
+    rr[0, zhi] = px[rows48(zlo), :] + rx2a[...] + rx2b[...] + rx2c[...]
+    c_x3 = [send(rr.at[0, zhi], rr.at[0, zhi], at_z(4 * e)) for e in (2, 1, 3)]
     arrived(c_z2)
     rr[1, zhi] = pz[x] + rz2[0] + rz2[1] + rz2[2]
     c_z3 = [send(rr.at[1, zhi], rr.at[1, zhi], at_z(4 * e)) for e in (2, 1, 3)]
-    arrived(c_x2)
-    rr[0, zhi] = px[rows48(zlo), :] + rx2a[...] + rx2b[...] + rx2c[...]
-    c_x3 = [send(rr.at[0, zhi], rr.at[0, zhi], at_z(4 * e)) for e in (2, 1, 3)]
-
-    arrived(c_g3)
-    gfull[mine] = g3[0] + g3[1] + g3[2] + g3[3]
-    c_g4 = [send(gfull.at[mine], gfull.at[mine], at_x(d)) for d in (2, 1, 3)]
-    arrived(c_g4)
-    four = gfull.at[pl.ds(4 * col, 4)]
-    c_g5 = [send(four, four, at_col(d)) for d in (4, 3, 5, 2, 6, 7, 1)]
     arrived(c_g5)
-
-    arrived(c_z3)
-    wz = rr[1, 0] + rr[1, 1] + rr[1, 2] + rr[1, 3]
-    mfz[x, rows48(zlo), :] = wz
-    own = mfz.at[x, rows48(zlo)]
-    c_z4 = [send(own, own, at_x(d)) for d in (2, 1, 3)]
-    arrived(c_x3)
-    mfx[x, rows48(zlo), :] = rr[0, 0] + rr[0, 1] + rr[0, 2] + rr[0, 3]
-
-    def own_rows(ref, at_rows):
-        whole, half_a, half_b = (at_rows(ref, rows) for rows in (rows48(zlo), rows24(zlo, 0), rows24(zlo, 1)))
-        return around_z(
-            lambda i: whole, lambda i: half_a, lambda i: half_b, (whole, whole), half_a, half_b
-        )
-
-    c_x4 = own_rows(mfx.at[x], lambda ref, rows: ref.at[rows])
 
     def block(i, j):
         if j == 2:
@@ -245,18 +233,25 @@
     l_ref[2] = block(2, 1) - dot_t(l20, l10)
     l_ref[3] = block(2, 2) - dot_t(l20, l20)
 
-    arrived(c_z4)
-    c_z5 = []
-    for half in (slice(0, 2), slice(2, 4)):
-        c_z5.append(own_rows(mfz.at[half], lambda ref, rows: ref.at[:, rows]))
-    arrived(c_x4)
-    c_x5 = [send(mfx.at[x], mfx.at[x], at_x(d)) for d in (2, 1, 3)]
-
     t11 = eliminate(s_ref)
     t_ref[64:128, 64:128] = t11
     l21 = dot_t(l_ref[2], t11)
     l_ref[2] = l21
     s_ref[...] = l_ref[3] - dot_t(l21, l21)
+
+    def own_rows(ref, at_rows):
+        whole, half_a, half_b = (at_rows(ref, rows) for rows in (rows48(zlo), rows24(zlo, 0), rows24(zlo, 1)))
+        return around_z(
+            lambda i: whole, lambda i: half_a, lambda i: half_b, (whole, whole), half_a, half_b
+        )
+
+    arrived(c_x3)
+    mfx[x, rows48(zlo), :] = rr[0, 0] + rr[0, 1] + rr[0, 2] + rr[0, 3]
+    c_x4 = own_rows(mfx.at[x], lambda ref, rows: ref.at[rows])
+    arrived(c_z3)
+    mfz[x, rows48(zlo), :] = rr[1, 0] + rr[1, 1] + rr[1, 2] + rr[1, 3]
+    own = mfz.at[x, rows48(zlo)]
+    c_z4 = [send(own, own, at_x(d)) for d in (2, 1, 3)]
 
     t22 = eliminate(s_ref)
     t00, t11 = t_ref[0:64, 0:64], t_ref[64:128, 64:128]
@@ -270,12 +265,16 @@
 
     norm_scale = 1.0 / math.sqrt(128 * 64)
 
+    arrived(c_z4)
+    c_z5 = [own_rows(mfz.at[q], lambda ref, rows: ref.at[rows]) for q in range(4)]
+    arrived(c_x4)
+    cx[x] = dot(t_ref[...], mfx[x])
+    c_x5 = [send(cx.at[x], cx.at[x], at_x(d)) for d in (2, 1, 3)]
     outs = []
 
-    def finish(chunk, first):
+    def finish(coeffs, first):
         i = len(outs) // 2
         cols = pl.ds(pl.multiple_of(first, 256), 256)
-        coeffs = dot(t_ref[...], chunk)
         r_buf[i] = coeffs * norm_scale
         outs.append(pltpu.make_async_copy(r_buf.at[i], r_out.at[:, cols], out_sem.at[2 * i]))
         outs[-1].start()
@@ -283,15 +282,14 @@
         outs.append(pltpu.make_async_copy(u_buf.at[i], u_out.at[:, cols], out_sem.at[2 * i + 1]))
         outs[-1].start()
 
-    finish(mfx[x], 256 * x)
-    for half in range(2):
-        arrived(c_z5[half])
-        for q in (2 * half, 2 * half + 1):
-            finish(mfz[q], 1024 + 256 * q)
+    finish(cx[x], 256 * x)
+    for q in range(4):
+        arrived(c_z5[q])
+        finish(dot(t_ref[...], mfz[q]), 1024 + 256 * q)
     for i, d in ((1, 1), (2, 3), (0, 2)):
         c_x5[i].wait_recv()
         chunk = (x + 4 - d) % 4
-        finish(mfx[chunk], 256 * chunk)
+        finish(cx[chunk], 256 * chunk)
 
     for copy in outs:
         copy.wait()
@@ -304,7 +302,7 @@
             panel_copy(col, d).wait_send()
 
 
-MESSAGES = 57
+MESSAGES = 78
 
 
 def on_device(slab):
@@ -323,10 +321,10 @@
         in_specs=[hbm],
         out_specs=(place, place),
         scratch_shapes=[
-            buf(128, 2048), buf(8, N, 256), buf(8, 128, 256), buf(N, 128), buf(32, 8, 128), buf(3, 8, 128), buf(4, 8, 128), buf(4, 8, 128), buf(32, 8, 128),
+            buf(128, 2048), buf(8, N, 256), buf(8, 128, 256), buf(N, 128), buf(32, 8, 128), buf(3, 8, 128), buf(16, 8, 128), buf(32, 8, 128),
             buf(4, N, 256), buf(N, 1024), buf(3, N, 256), buf(48, 1024), buf(48, 1024), buf(48, 1024),
             buf(N, 256), buf(4, 48, 256), buf(48, 256), buf(48, 256), buf(48, 256), buf(3, 48, 256),
-            buf(2, 4, 48, 256), buf(4, N, 256), buf(4, N, 256),
+            buf(2, 4, 48, 256), buf(4, N, 256), buf(4, N, 256), buf(4, N, 256),
             buf(64, 64), buf(4, 64, 64), buf(N, N), buf(128, N),
             pltpu.SemaphoreType.DMA((7,)), pltpu.SemaphoreType.DMA((PANELS,)),
             pltpu.SemaphoreType.DMA((MESSAGES,)), pltpu.SemaphoreType.DMA((MESSAGES,)),
@@ -334,7 +332,7 @@
             pltpu.SemaphoreType.REGULAR, pltpu.SemaphoreType.REGULAR,
         ],
         compiler_params=pltpu.CompilerParams(
-            collective_id=0, has_side_effects=True, vmem_limit_bytes=48 << 20
+            collective_id=0, has_side_effects=True, vmem_limit_bytes=63 << 20
         ),
     )(slab)
 

time: 82.4 us -> 78.1 us (0.948)
  the two profiles are of different devices: /device:TPU:1 before, /device:TPU:16 now
where the time goes in v3:
time: 78.1 us; the launch traced here: 77.9 us
  Pallas kernels  73.5 us (94%)
  local copies, waits for them, and re-layouts  3.76 us (5%)
    pallas_call x1, Pallas kernels, on_device(): pl.pallas_call(kernel, out_shape=(jax.ShapeDtypeStruct((N, 2048), F32), j...  73.5 us
    unnamed x4, local copies, waits for them, and re-layouts  3.76 us

profile of v3, /device:TPU:16, one launch (start us, length us, event | category | flops | bytes accessed | tf_op | source)
XLA Modules:
  0.0 77.9 jit_solution(5792638375962962958)
XLA Ops:
  0.6 73.5 %shard_map.30 = (f32[192,2048]{1,0:T(8,128)}, f32[128,2048]{1,0:T(8,128)}) custom-call(f32[128,2048]{1,0:T(8,128)} %slab_hbm.1), custom_call_target="tpu_custom_call" | custom-call | tf_op jit(solution)/shard_map/pallas_call | solution.py:315
  74.2 0.0 copy-start
  74.2 2.8 %copy.5 = f32[192,2048]{1,0:T(8,128)} copy(f32[192,2048]{1,0:T(8,128)} %get-tuple-element.4) | data formatting | bytes 3145728
  77.0 0.0 copy-done
  77.0 1.0 %copy.6 = f32[128,2048]{1,0:T(8,128)} copy(f32[128,2048]{1,0:T(8,128)S(1)} %copy-done) | data formatting | bytes 2097152
Async XLA Ops:
  74.2 2.8 %copy-start = (f32[128,2048]{1,0:T(8,128)S(1)}, f32[128,2048]{1,0:T(8,128)}, u32[]{:S(2)}) copy-start(f32[128,2048]{1,0:T(8,128)} %get-tuple-element.5) | copy-start | bytes 3145732

commit v4 on v3

--- a/solution.py
+++ b/solution.py
@@ -302,6 +302,17 @@
             panel_copy(col, d).wait_send()
 
 
+def write_out(r_in, u_in, r_out, u_out, sems):
+    copies = [
+        pltpu.make_async_copy(r_in, r_out, sems.at[0]),
+        pltpu.make_async_copy(u_in, u_out, sems.at[1]),
+    ]
+    for copy in copies:
+        copy.start()
+    for copy in copies:
+        copy.wait()
+
+
 MESSAGES = 78
 
 
@@ -312,7 +323,7 @@
     def buf(*shape):
         return pltpu.VMEM(shape, F32)
 
-    return pl.pallas_call(
+    results = pl.pallas_call(
         kernel,
         out_shape=(
             jax.ShapeDtypeStruct((N, 2048), F32),
@@ -332,9 +343,20 @@
             pltpu.SemaphoreType.REGULAR, pltpu.SemaphoreType.REGULAR,
         ],
         compiler_params=pltpu.CompilerParams(
-            collective_id=0, has_side_effects=True, vmem_limit_bytes=63 << 20
+            collective_id=0, has_side_effects=True, vmem_limit_bytes=50 << 20
         ),
     )(slab)
+    return pl.pallas_call(
+        write_out,
+        out_shape=(
+            jax.ShapeDtypeStruct((N, 2048), F32),
+            jax.ShapeDtypeStruct((128, 2048), F32),
+        ),
+        in_specs=[place, place],
+        out_specs=(place, place),
+        scratch_shapes=[pltpu.SemaphoreType.DMA((2,))],
+        compiler_params=pltpu.CompilerParams(vmem_limit_bytes=8 << 20),
+    )(*results)
 
 
 def solution(mesh):

time: 78.1 us -> 76.2 us (0.976)
  local copies, waits for them, and re-layouts: 3.76 us -> 1.22 us
    unnamed x4 -> x2, local copies, waits for them, and re-layouts: 3.76 us -> 1.22 us
    pallas_call x0 -> x1, Pallas kernels: none -> 1.51 us  [on_device(): pl.pallas_call(write_out, out_shape=(jax.ShapeDtypeStruct((N, 2048), F32)...]
    pallas_call x1, Pallas kernels: 73.5 us -> 72.7 us  [on_device(): pl.pallas_call(kernel, out_shape=(jax.ShapeDtypeStruct((N, 2048), F32), j...]
where the time goes in v4:
time: 76.2 us; the launch traced here: 76 us
  Pallas kernels  74.2 us (97%)
  local copies, waits for them, and re-layouts  1.22 us (2%)
    pallas_call x1, Pallas kernels, on_device(): pl.pallas_call(kernel, out_shape=(jax.ShapeDtypeStruct((N, 2048), F32), j...  72.7 us

profile of v4, /device:TPU:16, one launch (start us, length us, event | category | flops | bytes accessed | tf_op | source)
XLA Modules:
  0.0 76.0 jit_solution(5369737313626445983)
XLA Ops:
  0.6 0.0 copy-start
  0.6 1.2 %copy-done = f32[128,2048]{1,0:T(8,128)S(1)} copy-done((f32[128,2048]{1,0:T(8,128)S(1)}, f32[128,2048]{1,0:T(8,128)}, u32[]{:S(2)}) %copy-start) | copy-done | bytes 1048600
  1.9 72.7 %shard_map.30 = (f32[192,2048]{1,0:T(8,128)S(1)}, f32[128,2048]{1,0:T(8,128)S(1)}) custom-call(f32[128,2048]{1,0:T(8,128)S(1)} %copy-done), custom_call_target="tpu_custom_call" | custom-call | tf_op jit(solution)/shard_map/pallas_call | solution.py:326
  74.5 1.5 %shard_map.31 = (f32[192,2048]{1,0:T(8,128)}, f32[128,2048]{1,0:T(8,128)}) custom-call(f32[192,2048]{1,0:T(8,128)S(1)} %get-tuple-element.4.r_in, f32[128,2048]{1,0:T(8,128)S(1)} %get-tuple-element.5.u_in), custom_call_target="tpu_custom_call" | custom-call | tf_op jit(solution)/shard_map/pallas_call | solution.py:349
Async XLA Ops:
  0.6 1.2 %copy-start = (f32[128,2048]{1,0:T(8,128)S(1)}, f32[128,2048]{1,0:T(8,128)}, u32[]{:S(2)}) copy-start(f32[128,2048]{1,0:T(8,128)} %slab_hbm.1) | copy-start | bytes 3145732

commit v5 on v4

--- a/solution.py
+++ b/solution.py
@@ -162,60 +162,102 @@
     def rows24(i, half):
         return pl.ds(pl.multiple_of(48 * i + 24 * half, 8), 24)
 
-    def first_z(half):
-        for q in (2 * half, 2 * half + 1):
-            mz[:, 256 * q:256 * q + 256] = dot(panels_t, slab[:, 1024 + 256 * q:1280 + 256 * q])
-
-    def send_z(half):
-        cols = slice(512 * half, 512 * half + 512)
+    def x_products(h):
+        m = dot(panels_t, slab[:, 512 * h:512 * h + 512])
+        for q in range(4):
+            mx[h, q] = m[:, 128 * q:128 * q + 128]
+
+    def z_products(h):
+        mz[h] = dot(panels_t, slab[:, 1024 + 512 * h:1536 + 512 * h])
+
+    def x1(h):
+        return [send(mx.at[h, (x + d) % 4], rx1.at[h, d - 1], at_x(d)) for d in (2, 1, 3)]
+
+    def z1(h):
         return around_z(
-            lambda i: mz.at[rows48(i), cols], lambda i: mz.at[rows24(i, 0), cols],
-            lambda i: mz.at[rows24(i, 1), cols],
-            (rz1a.at[:, cols], rz1b.at[:, cols]), rz1c.at[0:24, cols], rz1c.at[24:48, cols],
+            lambda i: mz.at[h, rows48(i)], lambda i: mz.at[h, rows24(i, 0)], lambda i: mz.at[h, rows24(i, 1)],
+            (rz1a.at[h], rz1b.at[h]), rz1c.at[h, 0:24], rz1c.at[h, 24:48],
         )
 
-    first_z(0)
-    c_z1 = send_z(0)
-    c_x1 = []
-    for d in (2, 1, 3, 0):
-        chunk = (x + d) % 4
-        mx[chunk] = dot(panels_t, slab[:, pl.ds(pl.multiple_of(256 * chunk, 256), 256)])
-        if d:
-            c_x1.append(send(mx.at[chunk], rx1.at[d - 1], at_x(d)))
-    first_z(1)
-
+    def x2(h, before):
+        arrived(before)
+        px[h] = mx[h, x] + rx1[h, 0] + rx1[h, 1] + rx1[h, 2]
+        return around_z(
+            lambda i: px.at[h, rows48(i)], lambda i: px.at[h, rows24(i, 0)], lambda i: px.at[h, rows24(i, 1)],
+            (rx2a.at[h], rx2b.at[h]), rx2c.at[h, 0:24], rx2c.at[h, 24:48],
+        )
+
+    def z2(h, before):
+        arrived(before)
+        for q in range(4):
+            cols = slice(128 * q, 128 * q + 128)
+            pz[h, q] = mz[h, rows48(zlo), cols] + rz1a[h, :, cols] + rz1b[h, :, cols] + rz1c[h, :, cols]
+        return [send(pz.at[h, (x + d) % 4], rz2.at[h, d - 1], at_x(d)) for d in (2, 1, 3)]
+
+    def across_z(s):
+        return [send(rr.at[s, zhi], rr.at[s, zhi], at_z(4 * e)) for e in (2, 1, 3)]
+
+    def x3(h, before):
+        arrived(before)
+        rr[h, zhi] = px[h, rows48(zlo), :] + rx2a[h] + rx2b[h] + rx2c[h]
+        return across_z(h)
+
+    def z3(h, before):
+        arrived(before)
+        rr[2 + h, zhi] = pz[h, x] + rz2[h, 0] + rz2[h, 1] + rz2[h, 2]
+        return across_z(2 + h)
+
+    def own_rows(ref, at_rows):
+        whole, half_a, half_b = (at_rows(ref, rows) for rows in (rows48(zlo), rows24(zlo, 0), rows24(zlo, 1)))
+        return around_z(
+            lambda i: whole, lambda i: half_a, lambda i: half_b, (whole, whole), half_a, half_b
+        )
+
+    def x4(h, before):
+        arrived(before)
+        mfx[h, x, rows48(zlo), :] = rr[h, 0] + rr[h, 1] + rr[h, 2] + rr[h, 3]
+        return own_rows(mfx.at[h, x], lambda ref, rows: ref.at[rows])
+
+    def z4(h, before):
+        arrived(before)
+        mfz[h, x, rows48(zlo), :] = rr[2 + h, 0] + rr[2 + h, 1] + rr[2 + h, 2] + rr[2 + h, 3]
+        own = mfz.at[h, x, rows48(zlo)]
+        return [send(own, own, at_x(d)) for d in (2, 1, 3)]
+
+    def z5(h, before):
+        arrived(before)
+        return own_rows(mfz.at[h], lambda ref, rows: ref.at[:, rows])
+
+    z_products(0)
+    c_z1 = [z1(0)]
+    x_products(0)
+    c_x1 = [x1(0)]
+    x_products(1)
+    c_x1.append(x1(1))
+    z_products(1)
     arrived(c_g1)
     g2[z] = gp[mine] + g1[0] + g1[1] + g1[2]
     pl.semaphore_wait(far2, 2)
     c_g2 = [send(g2.at[z], g2.at[z], at_z(d)) for d in (8, 7, 9, 6, 10, 5, 11, 4, 12, 3, 13, 2, 14, 1, 15)]
-    c_z1 += send_z(1)
-
-    arrived(c_x1)
-    px[...] = mx[x] + rx1[0] + rx1[1] + rx1[2]
-    c_x2 = around_z(
-        lambda i: px.at[rows48(i)], lambda i: px.at[rows24(i, 0)], lambda i: px.at[rows24(i, 1)],
-        (rx2a, rx2b), rx2c.at[0:24], rx2c.at[24:48],
-    )
+    c_z1.append(z1(1))
+
+    c_z2 = [z2(0, c_z1[0])]
+    c_x2 = [x2(0, c_x1[0])]
+    c_x2.append(x2(1, c_x1[1]))
     arrived(c_g2)
     total = g2[0]
     for i in range(1, 16):
         total = total + g2[i]
     gfull[mine] = total
     c_g4 = [send(gfull.at[mine], gfull.at[mine], at_x(d)) for d in (2, 1, 3)]
-    arrived(c_z1)
-    for q in range(4):
-        cols = slice(256 * q, 256 * q + 256)
-        pz[q] = mz[rows48(zlo), cols] + rz1a[:, cols] + rz1b[:, cols] + rz1c[:, cols]
-    c_z2 = [send(pz.at[(x + d) % 4], rz2.at[d - 1], at_x(d)) for d in (2, 1, 3)]
+    c_z3 = [z3(0, c_z2[0])]
+    c_z2.append(z2(1, c_z1[1]))
+    c_x3 = [x3(0, c_x2[0])]
     arrived(c_g4)
     four = gfull.at[pl.ds(4 * col, 4)]
     c_g5 = [send(four, four, at_col(d)) for d in (4, 3, 5, 2, 6, 7, 1)]
-    arrived(c_x2)
-    rr[0, zhi] = px[rows48(zlo), :] + rx2a[...] + rx2b[...] + rx2c[...]
-    c_x3 = [send(rr.at[0, zhi], rr.at[0, zhi], at_z(4 * e)) for e in (2, 1, 3)]
-    arrived(c_z2)
-    rr[1, zhi] = pz[x] + rz2[0] + rz2[1] + rz2[2]
-    c_z3 = [send(rr.at[1, zhi], rr.at[1, zhi], at_z(4 * e)) for e in (2, 1, 3)]
+    c_x3.append(x3(1, c_x2[1]))
+    c_z3.append(z3(1, c_z2[1]))
     arrived(c_g5)
 
     def block(i, j):
@@ -233,48 +275,43 @@
     l_ref[2] = block(2, 1) - dot_t(l20, l10)
     l_ref[3] = block(2, 2) - dot_t(l20, l20)
 
+    c_z4 = [z4(0, c_z3[0])]
+
     t11 = eliminate(s_ref)
     t_ref[64:128, 64:128] = t11
     l21 = dot_t(l_ref[2], t11)
     l_ref[2] = l21
     s_ref[...] = l_ref[3] - dot_t(l21, l21)
 
-    def own_rows(ref, at_rows):
-        whole, half_a, half_b = (at_rows(ref, rows) for rows in (rows48(zlo), rows24(zlo, 0), rows24(zlo, 1)))
-        return around_z(
-            lambda i: whole, lambda i: half_a, lambda i: half_b, (whole, whole), half_a, half_b
-        )
-
-    arrived(c_x3)
-    mfx[x, rows48(zlo), :] = rr[0, 0] + rr[0, 1] + rr[0, 2] + rr[0, 3]
-    c_x4 = own_rows(mfx.at[x], lambda ref, rows: ref.at[rows])
-    arrived(c_z3)
-    mfz[x, rows48(zlo), :] = rr[1, 0] + rr[1, 1] + rr[1, 2] + rr[1, 3]
-    own = mfz.at[x, rows48(zlo)]
-    c_z4 = [send(own, own, at_x(d)) for d in (2, 1, 3)]
-
-    t22 = eliminate(s_ref)
-    t00, t11 = t_ref[0:64, 0:64], t_ref[64:128, 64:128]
+    c_x4 = [x4(0, c_x3[0])]
+
+    t_ref[128:192, 128:192] = eliminate(s_ref)
+
+    c_x4.append(x4(1, c_x3[1]))
+    c_z4.append(z4(1, c_z3[1]))
+    c_z5 = [z5(0, c_z4[0])]
+    arrived(c_x4[0])
+    c_x5 = [[send(mfx.at[0, x], mfx.at[0, x], at_x(d)) for d in (2, 1, 3)]]
+
+    t00, t11, t22 = (t_ref[i:i + 64, i:i + 64] for i in (0, 64, 128))
     l10, l20, l21 = l_ref[0], l_ref[1], l_ref[2]
     t10 = -dot(t11, dot(l10, t00))
     t_ref[64:128, 0:64] = t10
     t_ref[128:192, 0:64] = -dot(t22, dot(l20, t00) + dot(l21, t10))
     t_ref[128:192, 64:128] = -dot(t22, dot(l21, t11))
-    t_ref[128:192, 128:192] = t22
     q_ref[...] = dot(t_ref[...], at[...]).T
 
     norm_scale = 1.0 / math.sqrt(128 * 64)
 
-    arrived(c_z4)
-    c_z5 = [own_rows(mfz.at[q], lambda ref, rows: ref.at[rows]) for q in range(4)]
-    arrived(c_x4)
-    cx[x] = dot(t_ref[...], mfx[x])
-    c_x5 = [send(cx.at[x], cx.at[x], at_x(d)) for d in (2, 1, 3)]
+    arrived(c_x4[1])
+    cx[x] = dot(t_ref[...], mfx[1, x])
+    c_x5.append([send(cx.at[x], cx.at[x], at_x(d)) for d in (2, 1, 3)])
+    c_z5.append(z5(1, c_z4[1]))
     outs = []
 
     def finish(coeffs, first):
         i = len(outs) // 2
-        cols = pl.ds(pl.multiple_of(first, 256), 256)
+        cols = pl.ds(first, 256)
         r_buf[i] = coeffs * norm_scale
         outs.append(pltpu.make_async_copy(r_buf.at[i], r_out.at[:, cols], out_sem.at[2 * i]))
         outs[-1].start()
@@ -282,14 +319,21 @@
         outs.append(pltpu.make_async_copy(u_buf.at[i], u_out.at[:, cols], out_sem.at[2 * i + 1]))
         outs[-1].start()
 
-    finish(cx[x], 256 * x)
-    for q in range(4):
-        arrived(c_z5[q])
-        finish(dot(t_ref[...], mfz[q]), 1024 + 256 * q)
-    for i, d in ((1, 1), (2, 3), (0, 2)):
-        c_x5[i].wait_recv()
-        chunk = (x + 4 - d) % 4
-        finish(cx[chunk], 256 * chunk)
+    def finish_all(coeffs_of, chunks, first):
+        for q in (0, 2):
+            finish(coeffs_of(jnp.concatenate([chunks[q], chunks[q + 1]], 1)), first + 128 * q)
+
+    def from_products(m):
+        return dot(t_ref[...], m)
+
+    arrived(c_z5[0])
+    finish_all(from_products, [mfz[0, q] for q in range(4)], 1024)
+    arrived(c_x5[0])
+    finish_all(from_products, [mfx[0, q] for q in range(4)], 0)
+    arrived(c_x5[1])
+    finish_all(lambda coeffs: coeffs, [cx[q] for q in range(4)], 512)
+    arrived(c_z5[1])
+    finish_all(from_products, [mfz[1, q] for q in range(4)], 1536)
 
     for copy in outs:
         copy.wait()
@@ -313,7 +357,7 @@
         copy.wait()
 
 
-MESSAGES = 78
+MESSAGES = 96
 
 
 def on_device(slab):
@@ -333,9 +377,9 @@
         out_specs=(place, place),
         scratch_shapes=[
             buf(128, 2048), buf(8, N, 256), buf(8, 128, 256), buf(N, 128), buf(32, 8, 128), buf(3, 8, 128), buf(16, 8, 128), buf(32, 8, 128),
-            buf(4, N, 256), buf(N, 1024), buf(3, N, 256), buf(48, 1024), buf(48, 1024), buf(48, 1024),
-            buf(N, 256), buf(4, 48, 256), buf(48, 256), buf(48, 256), buf(48, 256), buf(3, 48, 256),
-            buf(2, 4, 48, 256), buf(4, N, 256), buf(4, N, 256), buf(4, N, 256),
+            buf(2, 4, N, 128), buf(2, N, 512), buf(2, 3, N, 128), buf(2, 48, 512), buf(2, 48, 512), buf(2, 48, 512),
+            buf(2, N, 128), buf(2, 4, 48, 128), buf(2, 48, 128), buf(2, 48, 128), buf(2, 48, 128), buf(2, 3, 48, 128),
+            buf(4, 4, 48, 128), buf(2, 4, N, 128), buf(2, 4, N, 128), buf(4, N, 128),
             buf(64, 64), buf(4, 64, 64), buf(N, N), buf(128, N),
             pltpu.SemaphoreType.DMA((7,)), pltpu.SemaphoreType.DMA((PANELS,)),
             pltpu.SemaphoreType.DMA((MESSAGES,)), pltpu.SemaphoreType.DMA((MESSAGES,)),

time: 76.2 us -> 73.9 us (0.970)
  the two profiles are of different devices: /device:TPU:16 before, /device:TPU:8 now
where the time goes in v5:
time: 73.9 us; the launch traced here: 73.7 us
  Pallas kernels  71.8 us (97%)
  local copies, waits for them, and re-layouts  1.22 us (2%)
    pallas_call x1, Pallas kernels, on_device(): pl.pallas_call(kernel, out_shape=(jax.ShapeDtypeStruct((N, 2048), F32), j...  70.3 us
    pallas_call x1, Pallas kernels, on_device(): pl.pallas_call(write_out, out_shape=(jax.ShapeDtypeStruct((N, 2048), F32)...  1.51 us

profile of v5, /device:TPU:8, one launch (start us, length us, event | category | flops | bytes accessed | tf_op | source)
XLA Modules:
  0.0 73.7 jit_solution(3640167274212181322)
XLA Ops:
  0.6 0.0 copy-start
  0.6 1.2 %copy-done = f32[128,2048]{1,0:T(8,128)S(1)} copy-done((f32[128,2048]{1,0:T(8,128)S(1)}, f32[128,2048]{1,0:T(8,128)}, u32[]{:S(2)}) %copy-start) | copy-done | bytes 1048600
  1.9 70.3 %shard_map.30 = (f32[192,2048]{1,0:T(8,128)S(1)}, f32[128,2048]{1,0:T(8,128)S(1)}) custom-call(f32[128,2048]{1,0:T(8,128)S(1)} %copy-done), custom_call_target="tpu_custom_call" | custom-call | tf_op jit(solution)/shard_map/pallas_call | solution.py:370
  72.2 1.5 %shard_map.31 = (f32[192,2048]{1,0:T(8,128)}, f32[128,2048]{1,0:T(8,128)}) custom-call(f32[192,2048]{1,0:T(8,128)S(1)} %get-tuple-element.4.r_in, f32[128,2048]{1,0:T(8,128)S(1)} %get-tuple-element.5.u_in), custom_call_target="tpu_custom_call" | custom-call | tf_op jit(solution)/shard_map/pallas_call | solution.py:393
Async XLA Ops:
  0.6 1.2 %copy-start = (f32[128,2048]{1,0:T(8,128)S(1)}, f32[128,2048]{1,0:T(8,128)}, u32[]{:S(2)}) copy-start(f32[128,2048]{1,0:T(8,128)} %slab_hbm.1) | copy-start | bytes 3145732

commit v6 on v5

--- a/solution.py
+++ b/solution.py
@@ -25,7 +25,7 @@
     return dot(a, b, ((1,), (1,)))
 
 
-def eliminate(s_ref):
+def eliminate(s_ref, begin, end):
     n = PANEL
     lane = lax.broadcasted_iota(jnp.int32, (n, n), 1)
     sub = lax.broadcasted_iota(jnp.int32, (n, n), 0)
@@ -61,16 +61,21 @@
         s_ref[...] = jnp.where(sub == j + 1, r1s, base - c0b * r0u - c1b * r1u)
         return 0
 
-    lax.fori_loop(0, n // 2, step, 0)
+    lax.fori_loop(begin // 2, end // 2, step, 0)
+
+
+def inverse_factor(s_ref):
+    lane = lax.broadcasted_iota(jnp.int32, (PANEL, PANEL), 1)
+    sub = lax.broadcasted_iota(jnp.int32, (PANEL, PANEL), 0)
     s = s_ref[...]
-    pivots = pick(s, lane == sub)
+    pivots = jnp.sum(jnp.where(lane == sub, s, 0.0), axis=1, keepdims=True)
     return jnp.where(lane < sub, s, jnp.where(lane == sub, 1.0, 0.0)) * (1.0 / jnp.sqrt(pivots))
 
 
 def kernel(
     slab_hbm, r_out, u_out,
     slab, r_buf, u_buf, at, gp, g1, g2, gfull,
-    mx, mz, rx1, rz1a, rz1b, rz1c, px, pz, rx2a, rx2b, rx2c, rz2, rr, mfx, mfz, cx,
+    mx, mz, rx1, rz1a, rz1b, rz1c, px, pz, rx2a, rx2b, rx2c, rz2, rr, mfx, mfz,
     s_ref, l_ref, t_ref, q_ref,
     p_send, p_recv, sends, recvs, in_sem, out_sem, far1, far2,
 ):
@@ -168,7 +173,7 @@
             mx[h, q] = m[:, 128 * q:128 * q + 128]
 
     def z_products(h):
-        mz[h] = dot(panels_t, slab[:, 1024 + 512 * h:1536 + 512 * h])
+        mz[h] = dot(panels_t, slab[:, 1536:2048])
 
     def x1(h):
         return [send(mx.at[h, (x + d) % 4], rx1.at[h, d - 1], at_x(d)) for d in (2, 1, 3)]
@@ -204,8 +209,8 @@
 
     def z3(h, before):
         arrived(before)
-        rr[2 + h, zhi] = pz[h, x] + rz2[h, 0] + rz2[h, 1] + rz2[h, 2]
-        return across_z(2 + h)
+        rr[3 + h, zhi] = pz[h, x] + rz2[h, 0] + rz2[h, 1] + rz2[h, 2]
+        return across_z(3 + h)
 
     def own_rows(ref, at_rows):
         whole, half_a, half_b = (at_rows(ref, rows) for rows in (rows48(zlo), rows24(zlo, 0), rows24(zlo, 1)))
@@ -220,7 +225,7 @@
 
     def z4(h, before):
         arrived(before)
-        mfz[h, x, rows48(zlo), :] = rr[2 + h, 0] + rr[2 + h, 1] + rr[2 + h, 2] + rr[2 + h, 3]
+        mfz[h, x, rows48(zlo), :] = rr[3 + h, 0] + rr[3 + h, 1] + rr[3 + h, 2] + rr[3 + h, 3]
         own = mfz.at[h, x, rows48(zlo)]
         return [send(own, own, at_x(d)) for d in (2, 1, 3)]
 
@@ -229,19 +234,17 @@
         return own_rows(mfz.at[h], lambda ref, rows: ref.at[:, rows])
 
     z_products(0)
-    c_z1 = [z1(0)]
-    x_products(0)
-    c_x1 = [x1(0)]
-    x_products(1)
-    c_x1.append(x1(1))
-    z_products(1)
+    c_z1 = z1(0)
+    c_x1 = []
+    for h in range(3):
+        x_products(h)
+        c_x1.append(x1(h))
     arrived(c_g1)
     g2[z] = gp[mine] + g1[0] + g1[1] + g1[2]
     pl.semaphore_wait(far2, 2)
     c_g2 = [send(g2.at[z], g2.at[z], at_z(d)) for d in (8, 7, 9, 6, 10, 5, 11, 4, 12, 3, 13, 2, 14, 1, 15)]
-    c_z1.append(z1(1))
-
-    c_z2 = [z2(0, c_z1[0])]
+
+    c_z2 = z2(0, c_z1)
     c_x2 = [x2(0, c_x1[0])]
     c_x2.append(x2(1, c_x1[1]))
     arrived(c_g2)
@@ -250,15 +253,19 @@
         total = total + g2[i]
     gfull[mine] = total
     c_g4 = [send(gfull.at[mine], gfull.at[mine], at_x(d)) for d in (2, 1, 3)]
-    c_z3 = [z3(0, c_z2[0])]
-    c_z2.append(z2(1, c_z1[1]))
     c_x3 = [x3(0, c_x2[0])]
+    c_x2.append(x2(2, c_x1[2]))
+    c_z3 = z3(0, c_z2)
+    c_x3.append(x3(1, c_x2[1]))
     arrived(c_g4)
     four = gfull.at[pl.ds(4 * col, 4)]
     c_g5 = [send(four, four, at_col(d)) for d in (4, 3, 5, 2, 6, 7, 1)]
-    c_x3.append(x3(1, c_x2[1]))
-    c_z3.append(z3(1, c_z2[1]))
+    c_x3.append(x3(2, c_x2[2]))
     arrived(c_g5)
+
+    def x5(h, before):
+        arrived(before)
+        return [send(mfx.at[h, x], mfx.at[h, x], at_x(d)) for d in (2, 1, 3)]
 
     def block(i, j):
         if j == 2:
@@ -267,7 +274,12 @@
 
     t_ref[...] = jnp.zeros_like(t_ref)
     s_ref[...] = block(0, 0)
-    t00 = eliminate(s_ref)
+    eliminate(s_ref, 0, 32)
+
+    c_x4 = [x4(0, c_x3[0])]
+
+    eliminate(s_ref, 32, 64)
+    t00 = inverse_factor(s_ref)
     l10, l20 = dot_t(block(1, 0), t00), dot_t(block(2, 0), t00)
     t_ref[0:64, 0:64] = t00
     l_ref[0], l_ref[1] = l10, l20
@@ -275,23 +287,27 @@
     l_ref[2] = block(2, 1) - dot_t(l20, l10)
     l_ref[3] = block(2, 2) - dot_t(l20, l20)
 
-    c_z4 = [z4(0, c_z3[0])]
-
-    t11 = eliminate(s_ref)
+    c_x4.append(x4(1, c_x3[1]))
+    c_z4 = z4(0, c_z3)
+
+    eliminate(s_ref, 0, 32)
+
+    c_x5 = [x5(0, c_x4[0])]
+
+    eliminate(s_ref, 32, 64)
+    t11 = inverse_factor(s_ref)
     t_ref[64:128, 64:128] = t11
     l21 = dot_t(l_ref[2], t11)
     l_ref[2] = l21
     s_ref[...] = l_ref[3] - dot_t(l21, l21)
 
-    c_x4 = [x4(0, c_x3[0])]
-
-    t_ref[128:192, 128:192] = eliminate(s_ref)
-
-    c_x4.append(x4(1, c_x3[1]))
-    c_z4.append(z4(1, c_z3[1]))
-    c_z5 = [z5(0, c_z4[0])]
-    arrived(c_x4[0])
-    c_x5 = [[send(mfx.at[0, x], mfx.at[0, x], at_x(d)) for d in (2, 1, 3)]]
+    c_x4.append(x4(2, c_x3[2]))
+    c_x5.append(x5(1, c_x4[1]))
+    c_z5 = z5(0, c_z4)
+
+    eliminate(s_ref, 0, 64)
+    t_ref[128:192, 128:192] = inverse_factor(s_ref)
+    c_x5.append(x5(2, c_x4[2]))
 
     t00, t11, t22 = (t_ref[i:i + 64, i:i + 64] for i in (0, 64, 128))
     l10, l20, l21 = l_ref[0], l_ref[1], l_ref[2]
@@ -303,10 +319,6 @@
 
     norm_scale = 1.0 / math.sqrt(128 * 64)
 
-    arrived(c_x4[1])
-    cx[x] = dot(t_ref[...], mfx[1, x])
-    c_x5.append([send(cx.at[x], cx.at[x], at_x(d)) for d in (2, 1, 3)])
-    c_z5.append(z5(1, c_z4[1]))
     outs = []
 
     def finish(coeffs, first):
@@ -319,21 +331,16 @@
         outs.append(pltpu.make_async_copy(u_buf.at[i], u_out.at[:, cols], out_sem.at[2 * i + 1]))
         outs[-1].start()
 
-    def finish_all(coeffs_of, chunks, first):
+    def finish_all(before, products, first):
+        arrived(before)
         for q in (0, 2):
-            finish(coeffs_of(jnp.concatenate([chunks[q], chunks[q + 1]], 1)), first + 128 * q)
-
-    def from_products(m):
-        return dot(t_ref[...], m)
-
-    arrived(c_z5[0])
-    finish_all(from_products, [mfz[0, q] for q in range(4)], 1024)
-    arrived(c_x5[0])
-    finish_all(from_products, [mfx[0, q] for q in range(4)], 0)
-    arrived(c_x5[1])
-    finish_all(lambda coeffs: coeffs, [cx[q] for q in range(4)], 512)
-    arrived(c_z5[1])
-    finish_all(from_products, [mfz[1, q] for q in range(4)], 1536)
+            pair = jnp.concatenate([products[q], products[q + 1]], 1)
+            finish(dot(t_ref[...], pair), first + 128 * q)
+
+    finish_all(c_x5[0], mfx.at[0], 0)
+    finish_all(c_z5, mfz.at[0], 1536)
+    finish_all(c_x5[1], mfx.at[1], 512)
+    finish_all(c_x5[2], mfx.at[2], 1024)
 
     for copy in outs:
         copy.wait()
@@ -377,9 +384,9 @@
         out_specs=(place, place),
         scratch_shapes=[
             buf(128, 2048), buf(8, N, 256), buf(8, 128, 256), buf(N, 128), buf(32, 8, 128), buf(3, 8, 128), buf(16, 8, 128), buf(32, 8, 128),
-            buf(2, 4, N, 128), buf(2, N, 512), buf(2, 3, N, 128), buf(2, 48, 512), buf(2, 48, 512), buf(2, 48, 512),
-            buf(2, N, 128), buf(2, 4, 48, 128), buf(2, 48, 128), buf(2, 48, 128), buf(2, 48, 128), buf(2, 3, 48, 128),
-            buf(4, 4, 48, 128), buf(2, 4, N, 128), buf(2, 4, N, 128), buf(4, N, 128),
+            buf(3, 4, N, 128), buf(1, N, 512), buf(3, 3, N, 128), buf(1, 48, 512), buf(1, 48, 512), buf(1, 48, 512),
+            buf(3, N, 128), buf(1, 4, 48, 128), buf(3, 48, 128), buf(3, 48, 128), buf(3, 48, 128), buf(1, 3, 48, 128),
+            buf(4, 4, 48, 128), buf(3, 4, N, 128), buf(1, 4, N, 128),
             buf(64, 64), buf(4, 64, 64), buf(N, N), buf(128, N),
             pltpu.SemaphoreType.DMA((7,)), pltpu.SemaphoreType.DMA((PANELS,)),
             pltpu.SemaphoreType.DMA((MESSAGES,)), pltpu.SemaphoreType.DMA((MESSAGES,)),

time: 73.9 us -> 74.5 us (level)
  the two profiles are of different devices: /device:TPU:8 before, /device:TPU:1 now
where the time goes in v6:
time: 74.5 us; the launch traced here: 74.3 us
  Pallas kernels  72.5 us (97%)
  local copies, waits for them, and re-layouts  1.22 us (2%)
    pallas_call x1, Pallas kernels, on_device(): pl.pallas_call(kernel, out_shape=(jax.ShapeDtypeStruct((N, 2048), F32), j...  71 us
    pallas_call x1, Pallas kernels, on_device(): pl.pallas_call(write_out, out_shape=(jax.ShapeDtypeStruct((N, 2048), F32)...  1.51 us

profile of v6, /device:TPU:1, one launch (start us, length us, event | category | flops | bytes accessed | tf_op | source)
XLA Modules:
  0.0 74.3 jit_solution(14050951508225756616)
XLA Ops:
  0.6 0.0 copy-start
  0.6 1.2 %copy-done = f32[128,2048]{1,0:T(8,128)S(1)} copy-done((f32[128,2048]{1,0:T(8,128)S(1)}, f32[128,2048]{1,0:T(8,128)}, u32[]{:S(2)}) %copy-start) | copy-done | bytes 1048600
  1.9 71.0 %shard_map.30 = (f32[192,2048]{1,0:T(8,128)S(1)}, f32[128,2048]{1,0:T(8,128)S(1)}) custom-call(f32[128,2048]{1,0:T(8,128)S(1)} %copy-done), custom_call_target="tpu_custom_call" | custom-call | tf_op jit(solution)/shard_map/pallas_call | solution.py:377
  72.8 1.5 %shard_map.31 = (f32[192,2048]{1,0:T(8,128)}, f32[128,2048]{1,0:T(8,128)}) custom-call(f32[192,2048]{1,0:T(8,128)S(1)} %get-tuple-element.4.r_in, f32[128,2048]{1,0:T(8,128)S(1)} %get-tuple-element.5.u_in), custom_call_target="tpu_custom_call" | custom-call | tf_op jit(solution)/shard_map/pallas_call | solution.py:400
Async XLA Ops:
  0.6 1.2 %copy-start = (f32[128,2048]{1,0:T(8,128)S(1)}, f32[128,2048]{1,0:T(8,128)}, u32[]{:S(2)}) copy-start(f32[128,2048]{1,0:T(8,128)} %slab_hbm.1) | copy-start | bytes 3145732

commit v7 on v6

--- a/solution.py
+++ b/solution.py
@@ -173,7 +173,7 @@
             mx[h, q] = m[:, 128 * q:128 * q + 128]
 
     def z_products(h):
-        mz[h] = dot(panels_t, slab[:, 1536:2048])
+        mz[h] = dot(panels_t, slab[:, 1024 + 512 * h:1536 + 512 * h])
 
     def x1(h):
         return [send(mx.at[h, (x + d) % 4], rx1.at[h, d - 1], at_x(d)) for d in (2, 1, 3)]
@@ -209,8 +209,8 @@
 
     def z3(h, before):
         arrived(before)
-        rr[3 + h, zhi] = pz[h, x] + rz2[h, 0] + rz2[h, 1] + rz2[h, 2]
-        return across_z(3 + h)
+        rr[2 + h, zhi] = pz[h, x] + rz2[h, 0] + rz2[h, 1] + rz2[h, 2]
+        return across_z(2 + h)
 
     def own_rows(ref, at_rows):
         whole, half_a, half_b = (at_rows(ref, rows) for rows in (rows48(zlo), rows24(zlo, 0), rows24(zlo, 1)))
@@ -225,26 +225,28 @@
 
     def z4(h, before):
         arrived(before)
-        mfz[h, x, rows48(zlo), :] = rr[3 + h, 0] + rr[3 + h, 1] + rr[3 + h, 2] + rr[3 + h, 3]
+        mfz[h, x, rows48(zlo), :] = rr[2 + h, 0] + rr[2 + h, 1] + rr[2 + h, 2] + rr[2 + h, 3]
         own = mfz.at[h, x, rows48(zlo)]
         return [send(own, own, at_x(d)) for d in (2, 1, 3)]
 
-    def z5(h, before):
-        arrived(before)
-        return own_rows(mfz.at[h], lambda ref, rows: ref.at[:, rows])
+    def z5(h, before, chunks):
+        arrived(before)
+        return own_rows(mfz.at[h, chunks], lambda ref, rows: ref.at[:, rows])
 
     z_products(0)
-    c_z1 = z1(0)
+    c_z1 = [z1(0)]
     c_x1 = []
-    for h in range(3):
+    for h in range(2):
         x_products(h)
         c_x1.append(x1(h))
+    z_products(1)
     arrived(c_g1)
     g2[z] = gp[mine] + g1[0] + g1[1] + g1[2]
     pl.semaphore_wait(far2, 2)
     c_g2 = [send(g2.at[z], g2.at[z], at_z(d)) for d in (8, 7, 9, 6, 10, 5, 11, 4, 12, 3, 13, 2, 14, 1, 15)]
-
-    c_z2 = z2(0, c_z1)
+    c_z1.append(z1(1))
+
+    c_z2 = [z2(0, c_z1[0])]
     c_x2 = [x2(0, c_x1[0])]
     c_x2.append(x2(1, c_x1[1]))
     arrived(c_g2)
@@ -253,14 +255,14 @@
         total = total + g2[i]
     gfull[mine] = total
     c_g4 = [send(gfull.at[mine], gfull.at[mine], at_x(d)) for d in (2, 1, 3)]
+    c_z3 = [z3(0, c_z2[0])]
+    c_z2.append(z2(1, c_z1[1]))
     c_x3 = [x3(0, c_x2[0])]
-    c_x2.append(x2(2, c_x1[2]))
-    c_z3 = z3(0, c_z2)
-    c_x3.append(x3(1, c_x2[1]))
     arrived(c_g4)
     four = gfull.at[pl.ds(4 * col, 4)]
     c_g5 = [send(four, four, at_col(d)) for d in (4, 3, 5, 2, 6, 7, 1)]
-    c_x3.append(x3(2, c_x2[2]))
+    c_x3.append(x3(1, c_x2[1]))
+    c_z3.append(z3(1, c_z2[1]))
     arrived(c_g5)
 
     def x5(h, before):
@@ -276,7 +278,7 @@
     s_ref[...] = block(0, 0)
     eliminate(s_ref, 0, 32)
 
-    c_x4 = [x4(0, c_x3[0])]
+    c_z4 = [z4(0, c_z3[0])]
 
     eliminate(s_ref, 32, 64)
     t00 = inverse_factor(s_ref)
@@ -287,12 +289,12 @@
     l_ref[2] = block(2, 1) - dot_t(l20, l10)
     l_ref[3] = block(2, 2) - dot_t(l20, l20)
 
+    c_x4 = [x4(0, c_x3[0])]
+
+    eliminate(s_ref, 0, 32)
+
     c_x4.append(x4(1, c_x3[1]))
-    c_z4 = z4(0, c_z3)
-
-    eliminate(s_ref, 0, 32)
-
-    c_x5 = [x5(0, c_x4[0])]
+    c_z5 = [z5(0, c_z4[0], slice(0, 4))]
 
     eliminate(s_ref, 32, 64)
     t11 = inverse_factor(s_ref)
@@ -301,13 +303,14 @@
     l_ref[2] = l21
     s_ref[...] = l_ref[3] - dot_t(l21, l21)
 
-    c_x4.append(x4(2, c_x3[2]))
+    c_x5 = [x5(0, c_x4[0])]
+    c_z4.append(z4(1, c_z3[1]))
     c_x5.append(x5(1, c_x4[1]))
-    c_z5 = z5(0, c_z4)
 
     eliminate(s_ref, 0, 64)
     t_ref[128:192, 128:192] = inverse_factor(s_ref)
-    c_x5.append(x5(2, c_x4[2]))
+    c_z5.append(z5(1, c_z4[1], slice(0, 2)))
+    c_z5.append(z5(1, [], slice(2, 4)))
 
     t00, t11, t22 = (t_ref[i:i + 64, i:i + 64] for i in (0, 64, 128))
     l10, l20, l21 = l_ref[0], l_ref[1], l_ref[2]
@@ -331,16 +334,19 @@
         outs.append(pltpu.make_async_copy(u_buf.at[i], u_out.at[:, cols], out_sem.at[2 * i + 1]))
         outs[-1].start()
 
-    def finish_all(before, products, first):
+    def finish_pair(products, q, first):
+        pair = jnp.concatenate([products[q], products[q + 1]], 1)
+        finish(dot(t_ref[...], pair), first + 128 * q)
+
+    for before, products, first in (
+        (c_x5[0], mfx.at[0], 0), (c_z5[0], mfz.at[0], 1024), (c_x5[1], mfx.at[1], 512)
+    ):
         arrived(before)
         for q in (0, 2):
-            pair = jnp.concatenate([products[q], products[q + 1]], 1)
-            finish(dot(t_ref[...], pair), first + 128 * q)
-
-    finish_all(c_x5[0], mfx.at[0], 0)
-    finish_all(c_z5, mfz.at[0], 1536)
-    finish_all(c_x5[1], mfx.at[1], 512)
-    finish_all(c_x5[2], mfx.at[2], 1024)
+            finish_pair(products, q, first)
+    for q in (0, 2):
+        arrived(c_z5[1 + q // 2])
+        finish_pair(mfz.at[1], q, 1536)
 
     for copy in outs:
         copy.wait()
@@ -364,7 +370,7 @@
         copy.wait()
 
 
-MESSAGES = 96
+MESSAGES = 100
 
 
 def on_device(slab):
@@ -384,9 +390,9 @@
         out_specs=(place, place),
         scratch_shapes=[
             buf(128, 2048), buf(8, N, 256), buf(8, 128, 256), buf(N, 128), buf(32, 8, 128), buf(3, 8, 128), buf(16, 8, 128), buf(32, 8, 128),
-            buf(3, 4, N, 128), buf(1, N, 512), buf(3, 3, N, 128), buf(1, 48, 512), buf(1, 48, 512), buf(1, 48, 512),
-            buf(3, N, 128), buf(1, 4, 48, 128), buf(3, 48, 128), buf(3, 48, 128), buf(3, 48, 128), buf(1, 3, 48, 128),
-            buf(4, 4, 48, 128), buf(3, 4, N, 128), buf(1, 4, N, 128),
+            buf(2, 4, N, 128), buf(2, N, 512), buf(2, 3, N, 128), buf(2, 48, 512), buf(2, 48, 512), buf(2, 48, 512),
+            buf(2, N, 128), buf(2, 4, 48, 128), buf(2, 48, 128), buf(2, 48, 128), buf(2, 48, 128), buf(2, 3, 48, 128),
+            buf(4, 4, 48, 128), buf(2, 4, N, 128), buf(2, 4, N, 128),
             buf(64, 64), buf(4, 64, 64), buf(N, N), buf(128, N),
             pltpu.SemaphoreType.DMA((7,)), pltpu.SemaphoreType.DMA((PANELS,)),
             pltpu.SemaphoreType.DMA((MESSAGES,)), pltpu.SemaphoreType.DMA((MESSAGES,)),

time: 74.5 us -> 74.9 us (level)
  the two profiles are of different devices: /device:TPU:1 before, /device:TPU:32 now
where the time goes in v7:
time: 74.9 us; the launch traced here: 74.8 us
  Pallas kernels  72.9 us (97%)
  local copies, waits for them, and re-layouts  1.22 us (2%)
    pallas_call x1, Pallas kernels, on_device(): pl.pallas_call(kernel, out_shape=(jax.ShapeDtypeStruct((N, 2048), F32), j...  71.4 us
    pallas_call x1, Pallas kernels, on_device(): pl.pallas_call(write_out, out_shape=(jax.ShapeDtypeStruct((N, 2048), F32)...  1.51 us

profile of v7, /device:TPU:32, one launch (start us, length us, event | category | flops | bytes accessed | tf_op | source)
XLA Modules:
  0.0 74.8 jit_solution(8326373658966394203)
XLA Ops:
  0.6 0.0 copy-start
  0.6 1.2 %copy-done = f32[128,2048]{1,0:T(8,128)S(1)} copy-done((f32[128,2048]{1,0:T(8,128)S(1)}, f32[128,2048]{1,0:T(8,128)}, u32[]{:S(2)}) %copy-start) | copy-done | bytes 1048600
  1.9 71.4 %shard_map.30 = (f32[192,2048]{1,0:T(8,128)S(1)}, f32[128,2048]{1,0:T(8,128)S(1)}) custom-call(f32[128,2048]{1,0:T(8,128)S(1)} %copy-done), custom_call_target="tpu_custom_call" | custom-call | tf_op jit(solution)/shard_map/pallas_call | solution.py:383
  73.3 1.5 %shard_map.31 = (f32[192,2048]{1,0:T(8,128)}, f32[128,2048]{1,0:T(8,128)}) custom-call(f32[192,2048]{1,0:T(8,128)S(1)} %get-tuple-element.4.r_in, f32[128,2048]{1,0:T(8,128)S(1)} %get-tuple-element.5.u_in), custom_call_target="tpu_custom_call" | custom-call | tf_op jit(solution)/shard_map/pallas_call | solution.py:406
Async XLA Ops:
  0.6 1.2 %copy-start = (f32[128,2048]{1,0:T(8,128)S(1)}, f32[128,2048]{1,0:T(8,128)}, u32[]{:S(2)}) copy-start(f32[128,2048]{1,0:T(8,128)} %slab_hbm.1) | copy-start | bytes 3145732

commit v8 on v7

--- a/solution.py
+++ b/solution.py
@@ -233,12 +233,12 @@
         arrived(before)
         return own_rows(mfz.at[h, chunks], lambda ref, rows: ref.at[:, rows])
 
+    x_products(0)
+    c_x1 = [x1(0)]
     z_products(0)
     c_z1 = [z1(0)]
-    c_x1 = []
-    for h in range(2):
-        x_products(h)
-        c_x1.append(x1(h))
+    x_products(1)
+    c_x1.append(x1(1))
     z_products(1)
     arrived(c_g1)
     g2[z] = gp[mine] + g1[0] + g1[1] + g1[2]
@@ -246,9 +246,10 @@
     c_g2 = [send(g2.at[z], g2.at[z], at_z(d)) for d in (8, 7, 9, 6, 10, 5, 11, 4, 12, 3, 13, 2, 14, 1, 15)]
     c_z1.append(z1(1))
 
+    c_x2 = [x2(0, c_x1[0])]
     c_z2 = [z2(0, c_z1[0])]
-    c_x2 = [x2(0, c_x1[0])]
     c_x2.append(x2(1, c_x1[1]))
+    c_x3 = [x3(0, c_x2[0])]
     arrived(c_g2)
     total = g2[0]
     for i in range(1, 16):
@@ -257,11 +258,10 @@
     c_g4 = [send(gfull.at[mine], gfull.at[mine], at_x(d)) for d in (2, 1, 3)]
     c_z3 = [z3(0, c_z2[0])]
     c_z2.append(z2(1, c_z1[1]))
-    c_x3 = [x3(0, c_x2[0])]
+    c_x3.append(x3(1, c_x2[1]))
     arrived(c_g4)
     four = gfull.at[pl.ds(4 * col, 4)]
     c_g5 = [send(four, four, at_col(d)) for d in (4, 3, 5, 2, 6, 7, 1)]
-    c_x3.append(x3(1, c_x2[1]))
     c_z3.append(z3(1, c_z2[1]))
     arrived(c_g5)
 
@@ -278,6 +278,7 @@
     s_ref[...] = block(0, 0)
     eliminate(s_ref, 0, 32)
 
+    c_x4 = [x4(0, c_x3[0])]
     c_z4 = [z4(0, c_z3[0])]
 
     eliminate(s_ref, 32, 64)
@@ -289,12 +290,13 @@
     l_ref[2] = block(2, 1) - dot_t(l20, l10)
     l_ref[3] = block(2, 2) - dot_t(l20, l20)
 
-    c_x4 = [x4(0, c_x3[0])]
+    c_x4.append(x4(1, c_x3[1]))
+    c_x5 = [x5(0, c_x4[0])]
+    c_z5 = [z5(0, c_z4[0], slice(0, 4))]
 
     eliminate(s_ref, 0, 32)
 
-    c_x4.append(x4(1, c_x3[1]))
-    c_z5 = [z5(0, c_z4[0], slice(0, 4))]
+    c_z4.append(z4(1, c_z3[1]))
 
     eliminate(s_ref, 32, 64)
     t11 = inverse_factor(s_ref)
@@ -303,14 +305,15 @@
     l_ref[2] = l21
     s_ref[...] = l_ref[3] - dot_t(l21, l21)
 
-    c_x5 = [x5(0, c_x4[0])]
-    c_z4.append(z4(1, c_z3[1]))
     c_x5.append(x5(1, c_x4[1]))
 
-    eliminate(s_ref, 0, 64)
-    t_ref[128:192, 128:192] = inverse_factor(s_ref)
+    eliminate(s_ref, 0, 32)
+
     c_z5.append(z5(1, c_z4[1], slice(0, 2)))
     c_z5.append(z5(1, [], slice(2, 4)))
+
+    eliminate(s_ref, 32, 64)
+    t_ref[128:192, 128:192] = inverse_factor(s_ref)
 
     t00, t11, t22 = (t_ref[i:i + 64, i:i + 64] for i in (0, 64, 128))
     l10, l20, l21 = l_ref[0], l_ref[1], l_ref[2]

time: 74.9 us -> 76.5 us (1.021)
  the two profiles are of different devices: /device:TPU:32 before, /device:TPU:8 now
where the time goes in v8:
time: 76.5 us; the launch traced here: 76.3 us
  Pallas kernels  74.4 us (97%)
  local copies, waits for them, and re-layouts  1.22 us (2%)
    pallas_call x1, Pallas kernels, on_device(): pl.pallas_call(kernel, out_shape=(jax.ShapeDtypeStruct((N, 2048), F32), j...  72.9 us

profile of v8, /device:TPU:8, one launch (start us, length us, event | category | flops | bytes accessed | tf_op | source)
XLA Modules:
  0.0 76.3 jit_solution(17519293299677693638)
XLA Ops:
  0.6 0.0 copy-start
  0.6 1.2 %copy-done = f32[128,2048]{1,0:T(8,128)S(1)} copy-done((f32[128,2048]{1,0:T(8,128)S(1)}, f32[128,2048]{1,0:T(8,128)}, u32[]{:S(2)}) %copy-start) | copy-done | bytes 1048600
  1.9 72.9 %shard_map.30 = (f32[192,2048]{1,0:T(8,128)S(1)}, f32[128,2048]{1,0:T(8,128)S(1)}) custom-call(f32[128,2048]{1,0:T(8,128)S(1)} %copy-done), custom_call_target="tpu_custom_call" | custom-call | tf_op jit(solution)/shard_map/pallas_call | solution.py:386
  74.8 1.5 %shard_map.31 = (f32[192,2048]{1,0:T(8,128)}, f32[128,2048]{1,0:T(8,128)}) custom-call(f32[192,2048]{1,0:T(8,128)S(1)} %get-tuple-element.4.r_in, f32[128,2048]{1,0:T(8,128)S(1)} %get-tuple-element.5.u_in), custom_call_target="tpu_custom_call" | custom-call | tf_op jit(solution)/shard_map/pallas_call | solution.py:409
Async XLA Ops:
  0.6 1.2 %copy-start = (f32[128,2048]{1,0:T(8,128)S(1)}, f32[128,2048]{1,0:T(8,128)}, u32[]{:S(2)}) copy-start(f32[128,2048]{1,0:T(8,128)} %slab_hbm.1) | copy-start | bytes 3145732

commit v9 on v5

--- a/solution.py
+++ b/solution.py
@@ -70,7 +70,7 @@
 def kernel(
     slab_hbm, r_out, u_out,
     slab, r_buf, u_buf, at, gp, g1, g2, gfull,
-    mx, mz, rx1, rz1a, rz1b, rz1c, px, pz, rx2a, rx2b, rx2c, rz2, rr, mfx, mfz, cx,
+    mx, mz, rx1, rz1a, rz1b, rz1c, px, pz, rx2a, rx2b, rx2c, rz2, rr, mfx, mfz,
     s_ref, l_ref, t_ref, q_ref,
     p_send, p_recv, sends, recvs, in_sem, out_sem, far1, far2,
 ):
@@ -289,9 +289,11 @@
 
     c_x4.append(x4(1, c_x3[1]))
     c_z4.append(z4(1, c_z3[1]))
-    c_z5 = [z5(0, c_z4[0])]
     arrived(c_x4[0])
     c_x5 = [[send(mfx.at[0, x], mfx.at[0, x], at_x(d)) for d in (2, 1, 3)]]
+    c_z5 = [z5(0, c_z4[0])]
+    arrived(c_x4[1])
+    c_x5.append([send(mfx.at[1, x], mfx.at[1, x], at_x(d)) for d in (2, 1, 3)])
 
     t00, t11, t22 = (t_ref[i:i + 64, i:i + 64] for i in (0, 64, 128))
     l10, l20, l21 = l_ref[0], l_ref[1], l_ref[2]
@@ -303,9 +305,6 @@
 
     norm_scale = 1.0 / math.sqrt(128 * 64)
 
-    arrived(c_x4[1])
-    cx[x] = dot(t_ref[...], mfx[1, x])
-    c_x5.append([send(cx.at[x], cx.at[x], at_x(d)) for d in (2, 1, 3)])
     c_z5.append(z5(1, c_z4[1]))
     outs = []
 
@@ -319,21 +318,16 @@
         outs.append(pltpu.make_async_copy(u_buf.at[i], u_out.at[:, cols], out_sem.at[2 * i + 1]))
         outs[-1].start()
 
-    def finish_all(coeffs_of, chunks, first):
+    def finish_all(before, products, first):
+        arrived(before)
         for q in (0, 2):
-            finish(coeffs_of(jnp.concatenate([chunks[q], chunks[q + 1]], 1)), first + 128 * q)
-
-    def from_products(m):
-        return dot(t_ref[...], m)
-
-    arrived(c_z5[0])
-    finish_all(from_products, [mfz[0, q] for q in range(4)], 1024)
-    arrived(c_x5[0])
-    finish_all(from_products, [mfx[0, q] for q in range(4)], 0)
-    arrived(c_x5[1])
-    finish_all(lambda coeffs: coeffs, [cx[q] for q in range(4)], 512)
-    arrived(c_z5[1])
-    finish_all(from_products, [mfz[1, q] for q in range(4)], 1536)
+            pair = jnp.concatenate([products[q], products[q + 1]], 1)
+            finish(dot(t_ref[...], pair), first + 128 * q)
+
+    finish_all(c_x5[0], mfx.at[0], 0)
+    finish_all(c_z5[0], mfz.at[0], 1024)
+    finish_all(c_x5[1], mfx.at[1], 512)
+    finish_all(c_z5[1], mfz.at[1], 1536)
 
     for copy in outs:
         copy.wait()
@@ -379,7 +373,7 @@
             buf(128, 2048), buf(8, N, 256), buf(8, 128, 256), buf(N, 128), buf(32, 8, 128), buf(3, 8, 128), buf(16, 8, 128), buf(32, 8, 128),
             buf(2, 4, N, 128), buf(2, N, 512), buf(2, 3, N, 128), buf(2, 48, 512), buf(2, 48, 512), buf(2, 48, 512),
             buf(2, N, 128), buf(2, 4, 48, 128), buf(2, 48, 128), buf(2, 48, 128), buf(2, 48, 128), buf(2, 3, 48, 128),
-            buf(4, 4, 48, 128), buf(2, 4, N, 128), buf(2, 4, N, 128), buf(4, N, 128),
+            buf(4, 4, 48, 128), buf(2, 4, N, 128), buf(2, 4, N, 128),
             buf(64, 64), buf(4, 64, 64), buf(N, N), buf(128, N),
             pltpu.SemaphoreType.DMA((7,)), pltpu.SemaphoreType.DMA((PANELS,)),
             pltpu.SemaphoreType.DMA((MESSAGES,)), pltpu.SemaphoreType.DMA((MESSAGES,)),

time: 73.9 us -> 74.3 us (level)
  no operation moved by 1% of the time
where the time goes in v9:
time: 74.3 us; the launch traced here: 74.2 us
  Pallas kernels  72.3 us (97%)
  local copies, waits for them, and re-layouts  1.22 us (2%)
    pallas_call x1, Pallas kernels, on_device(): pl.pallas_call(kernel, out_shape=(jax.ShapeDtypeStruct((N, 2048), F32), j...  70.8 us
    pallas_call x1, Pallas kernels, on_device(): pl.pallas_call(write_out, out_shape=(jax.ShapeDtypeStruct((N, 2048), F32)...  1.51 us

profile of v9, /device:TPU:8, one launch (start us, length us, event | category | flops | bytes accessed | tf_op | source)
XLA Modules:
  0.0 74.2 jit_solution(6108086245569246478)
XLA Ops:
  0.6 0.0 copy-start
  0.6 1.2 %copy-done = f32[128,2048]{1,0:T(8,128)S(1)} copy-done((f32[128,2048]{1,0:T(8,128)S(1)}, f32[128,2048]{1,0:T(8,128)}, u32[]{:S(2)}) %copy-start) | copy-done | bytes 1048600
  1.9 70.8 %shard_map.30 = (f32[192,2048]{1,0:T(8,128)S(1)}, f32[128,2048]{1,0:T(8,128)S(1)}) custom-call(f32[128,2048]{1,0:T(8,128)S(1)} %copy-done), custom_call_target="tpu_custom_call" | custom-call | tf_op jit(solution)/shard_map/pallas_call | solution.py:364
  72.7 1.5 %shard_map.31 = (f32[192,2048]{1,0:T(8,128)}, f32[128,2048]{1,0:T(8,128)}) custom-call(f32[192,2048]{1,0:T(8,128)S(1)} %get-tuple-element.4.r_in, f32[128,2048]{1,0:T(8,128)S(1)} %get-tuple-element.5.u_in), custom_call_target="tpu_custom_call" | custom-call | tf_op jit(solution)/shard_map/pallas_call | solution.py:387
Async XLA Ops:
  0.6 1.2 %copy-start = (f32[128,2048]{1,0:T(8,128)S(1)}, f32[128,2048]{1,0:T(8,128)}, u32[]{:S(2)}) copy-start(f32[128,2048]{1,0:T(8,128)} %slab_hbm.1) | copy-start | bytes 3145732

commit v10 on v5

--- a/solution.py
+++ b/solution.py
@@ -224,9 +224,9 @@
         own = mfz.at[h, x, rows48(zlo)]
         return [send(own, own, at_x(d)) for d in (2, 1, 3)]
 
-    def z5(h, before):
-        arrived(before)
-        return own_rows(mfz.at[h], lambda ref, rows: ref.at[:, rows])
+    def z5(h, before, chunks):
+        arrived(before)
+        return own_rows(mfz.at[h, chunks], lambda ref, rows: ref.at[:, rows])
 
     z_products(0)
     c_z1 = [z1(0)]
@@ -289,7 +289,7 @@
 
     c_x4.append(x4(1, c_x3[1]))
     c_z4.append(z4(1, c_z3[1]))
-    c_z5 = [z5(0, c_z4[0])]
+    c_z5 = [z5(0, c_z4[0], slice(0, 4))]
     arrived(c_x4[0])
     c_x5 = [[send(mfx.at[0, x], mfx.at[0, x], at_x(d)) for d in (2, 1, 3)]]
 
@@ -306,7 +306,8 @@
     arrived(c_x4[1])
     cx[x] = dot(t_ref[...], mfx[1, x])
     c_x5.append([send(cx.at[x], cx.at[x], at_x(d)) for d in (2, 1, 3)])
-    c_z5.append(z5(1, c_z4[1]))
+    c_z5.append(z5(1, c_z4[1], slice(0, 2)))
+    c_z5.append(z5(1, [], slice(2, 4)))
     outs = []
 
     def finish(coeffs, first):
@@ -332,8 +333,9 @@
     finish_all(from_products, [mfx[0, q] for q in range(4)], 0)
     arrived(c_x5[1])
     finish_all(lambda coeffs: coeffs, [cx[q] for q in range(4)], 512)
-    arrived(c_z5[1])
-    finish_all(from_products, [mfz[1, q] for q in range(4)], 1536)
+    for q in (0, 2):
+        arrived(c_z5[1 + q // 2])
+        finish(from_products(jnp.concatenate([mfz[1, q], mfz[1, q + 1]], 1)), 1536 + 128 * q)
 
     for copy in outs:
         copy.wait()
@@ -357,7 +359,7 @@
         copy.wait()
 
 
-MESSAGES = 96
+MESSAGES = 100
 
 
 def on_device(slab):

time: 73.9 us -> 74 us (level)
  no operation moved by 1% of the time
where the time goes in v10:
time: 74 us; the launch traced here: 73.9 us
  Pallas kernels  72 us (97%)
  local copies, waits for them, and re-layouts  1.22 us (2%)
    pallas_call x1, Pallas kernels, on_device(): pl.pallas_call(kernel, out_shape=(jax.ShapeDtypeStruct((N, 2048), F32), j...  70.5 us
    pallas_call x1, Pallas kernels, on_device(): pl.pallas_call(write_out, out_shape=(jax.ShapeDtypeStruct((N, 2048), F32)...  1.51 us

profile of v10, /device:TPU:8, one launch (start us, length us, event | category | flops | bytes accessed | tf_op | source)
XLA Modules:
  0.0 73.9 jit_solution(4662517308270330305)
XLA Ops:
  0.6 0.0 copy-start
  0.6 1.2 %copy-done = f32[128,2048]{1,0:T(8,128)S(1)} copy-done((f32[128,2048]{1,0:T(8,128)S(1)}, f32[128,2048]{1,0:T(8,128)}, u32[]{:S(2)}) %copy-start) | copy-done | bytes 1048600
  1.9 70.5 %shard_map.30 = (f32[192,2048]{1,0:T(8,128)S(1)}, f32[128,2048]{1,0:T(8,128)S(1)}) custom-call(f32[128,2048]{1,0:T(8,128)S(1)} %copy-done), custom_call_target="tpu_custom_call" | custom-call | tf_op jit(solution)/shard_map/pallas_call | solution.py:372
  72.4 1.5 %shard_map.31 = (f32[192,2048]{1,0:T(8,128)}, f32[128,2048]{1,0:T(8,128)}) custom-call(f32[192,2048]{1,0:T(8,128)S(1)} %get-tuple-element.4.r_in, f32[128,2048]{1,0:T(8,128)S(1)} %get-tuple-element.5.u_in), custom_call_target="tpu_custom_call" | custom-call | tf_op jit(solution)/shard_map/pallas_call | solution.py:395
Async XLA Ops:
  0.6 1.2 %copy-start = (f32[128,2048]{1,0:T(8,128)S(1)}, f32[128,2048]{1,0:T(8,128)}, u32[]{:S(2)}) copy-start(f32[128,2048]{1,0:T(8,128)} %slab_hbm.1) | copy-start | bytes 3145732
